TPU v7x, 32 devices: a whole 2x2x4 slice. The times are simulated.
32 devices in a mesh: row: 4 (over z), chan: 8 (over y, x, core).
Axes of the slice: x: 2, y: 2, z: 4, core: 2. Of those that a mesh axis runs over, the one named last changes fastest.
Arguments:
- pair: bfloat16 [256, 256, 128], P('row', 'chan'), may hold values from -6 to 6
- tile_mask: int32 [64, 64], replicated, may hold values from 0 to 1, as said below
- in_gain: float32 [128], replicated, may hold values from 0.5 to 1.5
- in_shift: float32 [128], replicated, may hold values from -3 to 3
- left_gate: bfloat16 [128, 128], replicated, may hold values from -0.5 to 0.5
- left_proj: bfloat16 [128, 128], replicated, may hold values from -0.5 to 0.5
- right_gate: bfloat16 [128, 128], replicated, may hold values from -0.5 to 0.5
- right_proj: bfloat16 [128, 128], replicated, may hold values from -0.5 to 0.5
- out_gain: float32 [128], replicated, may hold values from 0.5 to 1.5
- out_shift: float32 [128], replicated, may hold values from -3 to 3
- out_gate: bfloat16 [128, 128], replicated, may hold values from -0.5 to 0.5
- out_proj: bfloat16 [128, 128], replicated, may hold values from -0.5 to 0.5
Outputs:
- updated: bfloat16 [256, 256, 128], P('row', 'chan')
Inputs may be any that keep to these rules, and one draw needn't show every extreme that they name: tile_mask[p, q] = valid[p] * valid[q] for a 0/1 vector valid over the 64 tiles that is 1 on the first 32 tiles and, in the second half, 1 on a leading run of 16 to 32 tiles and 0 after it.
All inputs are finite; a program needn't handle non-finite values.
Results may differ from a plain program's by a relative error of at most 0.012.
Values may be sent and summed in bfloat16 or wider, within the bound.
A program may use at most 64 MiB of HBM per device.

v0:
```python
import jax
import jax.numpy as jnp
from jax import lax
from jax.sharding import PartitionSpec as P

epsilon = 1e-05


def norm_last(values, gain, shift):
    average = jnp.mean(values, axis=-1, keepdims=True)
    squares = jnp.mean(values * values, axis=-1, keepdims=True)
    return (values - average) * lax.rsqrt(squares - average * average + epsilon) * gain + shift


def norm_first(values, gain, shift):
    average = jnp.mean(values, axis=0)
    squares = jnp.mean(values * values, axis=0)
    scaled = (values - average) * lax.rsqrt(squares - average * average + epsilon)
    return scaled * gain[:, None, None] + shift[:, None, None]


def local(
    pair,
    tile_mask,
    in_gain,
    in_shift,
    left_gate,
    left_proj,
    right_gate,
    right_proj,
    out_gain,
    out_shift,
    out_gate,
    out_proj,
):
    row_count, col_count, channels = pair.shape
    tile_count = tile_mask.shape[0]
    total_rows = row_count * lax.axis_size("row")
    tile_size = total_rows // tile_count
    row_start = lax.axis_index("row") * row_count
    col_start = lax.axis_index("chan") * col_count
    mask_f = tile_mask.astype(jnp.float32)
    tile_ids = jnp.arange(tile_count, dtype=jnp.int32)
    row_hot = (
        ((row_start + jnp.arange(row_count, dtype=jnp.int32)) // tile_size)[:, None]
        == tile_ids[None, :]
    ).astype(jnp.float32)
    col_hot = (
        ((col_start + jnp.arange(col_count, dtype=jnp.int32)) // tile_size)[:, None]
        == tile_ids[None, :]
    ).astype(jnp.float32)
    pair_mask = jnp.dot(
        jnp.dot(row_hot, mask_f, preferred_element_type=jnp.float32),
        col_hot.T,
        preferred_element_type=jnp.float32,
    )
    normed = norm_last(pair.astype(jnp.float32), in_gain, in_shift).astype(jnp.bfloat16)

    def edges(gate_w, proj_w):
        gate_pre = jnp.einsum("ijc,ch->hij", normed, gate_w, preferred_element_type=jnp.float32)
        proj_pre = jnp.einsum("ijc,ch->hij", normed, proj_w, preferred_element_type=jnp.float32)
        return (pair_mask[None] * jax.nn.sigmoid(gate_pre) * proj_pre).astype(jnp.bfloat16)

    left = edges(left_gate, left_proj)
    right = edges(right_gate, right_proj)
    left_x, right_x = (
        lax.all_to_all(left, "chan", split_axis=0, concat_axis=2, tiled=True),
        lax.all_to_all(right, "chan", split_axis=0, concat_axis=2, tiled=True),
    )
    partial_x = jnp.einsum(
        "hik,hjk->hij",
        left_x,
        lax.all_gather(right_x, "row", axis=1, tiled=True),
        preferred_element_type=jnp.float32,
    )
    crossed_b = partial_x.astype(jnp.bfloat16)
    crossed_back = lax.all_to_all(crossed_b, "chan", split_axis=2, concat_axis=0, tiled=True)
    normed_x = norm_first(crossed_back.astype(jnp.float32), out_gain, out_shift).astype(
        jnp.bfloat16
    )
    gating = jax.nn.sigmoid(
        jnp.einsum("ijc,cd->ijd", normed, out_gate, preferred_element_type=jnp.float32)
    )
    projected = jnp.einsum("hij,hd->ijd", normed_x, out_proj, preferred_element_type=jnp.float32)
    return (gating * projected).astype(jnp.bfloat16)


def solution(mesh):
    placed = (P("row", "chan", None), P(), P(), P(), P(), P(), P(), P(), P(), P(), P(), P())
    return jax.shard_map(
        local, mesh=mesh, in_specs=placed, out_specs=P("row", "chan", None), check_vma=False
    )
```

profile of v0, /device:TPU:0, one launch (start us, length us, event | category | flops | bytes accessed | tf_op | source)
XLA Modules:
  0.0 107.3 jit_solution(11398354881090640035)
XLA Ops:
  6.6 1.7 %convert_reduce_fusion = (f32[64,32]{1,0:T(8,128)S(1)}, f32[64,32]{1,0:T(8,128)S(1)}) fusion(bf16[64,32,128]{2,1,0:T(8,128)(2,1)} %param.12), kind=kLoop, calls=%fused_computation.9 | loop fusion | flops 1044480 | bytes 540672 | tf_op jit(solution)/shard_map/reduce_sum | solution.py:10
  8.5 0.1 copy.60
  8.7 1.1 fusion.23
  9.8 1.8 %fusion.34 = f32[64,32,128]{2,1,0:T(8,128)S(1)} fusion(bf16[128,128]{1,0:T(8,128)(2,1)S(1)} %copy-done, bf16[64,32,128]{2,1,0:T(8,128)(2,1)} %param.12, f32[128]{0:T(128)} %param.15, f32[128]{0:T(128)} %param.14, f32[64,32]{1,0:T(8,128)S(1)} %copy.62, f32[64,32]{1,0:T(8,128)S(1)} %copy.60), kind=kOutput, calls=%fused_computation.43 | convolution fusion | flops 68681728 | bytes 1623040 | tf_op jit(solution)/shard_map/ijc,ch->hij/dot_general | solution.py:61
  11.6 1.0 fusion.22
  12.6 1.7 %copy.66 = bf16[128,64,32]{1,2,0:T(8,128)(2,1)S(1)} copy(bf16[128,64,32]{0,2,1:T(8,128)(2,1)S(1)} %fusion.22) | data formatting | bytes 1048576 | tf_op jit(solution)/shard_map/convert_element_type | solution.py:62
  14.3 0.7 reshape.90
  15.0 14.7 %all_to_all.45 = bf16[8,2,16384]{2,1,0:T(2,128)(2,1)S(1)} all-to-all(bf16[8,2,16384]{2,1,0:T(2,128)(2,1)S(1)} %reshape.90), channel_id=1, replica_groups=mesh['row'=4,'chan'=8] {'chan'}, dimensions={0} | all-to-all | bytes 1048576 | tf_op jit(solution)/shard_map/all_to_all | solution.py:68
  29.7 0.7 reshape.91
  30.4 0.1 copy.67
  30.5 1.1 %copy.68 = bf16[16,64,256]{2,1,0:T(8,128)(2,1)} copy(bf16[16,64,256]{1,2,0:T(8,128)(2,1)S(1)} %bitcast.63) | data formatting | bytes 1048576 | tf_op jit(solution)/shard_map/all_to_all | solution.py:68
  31.7 0.7 fusion.37
  32.4 1.0 fusion.21
  33.4 1.7 %copy.64 = bf16[128,64,32]{1,2,0:T(8,128)(2,1)S(1)} copy(bf16[128,64,32]{0,2,1:T(8,128)(2,1)S(1)} %fusion.21) | data formatting | bytes 1048576 | tf_op jit(solution)/shard_map/convert_element_type | solution.py:62
  35.1 0.7 reshape.88
  35.9 12.2 %all_to_all.46 = bf16[8,2,16384]{2,1,0:T(2,128)(2,1)S(1)} all-to-all(bf16[8,2,16384]{2,1,0:T(2,128)(2,1)S(1)} %reshape.88), channel_id=1, replica_groups=mesh['row'=4,'chan'=8] {'chan'}, dimensions={0} | all-to-all | bytes 1048576 | tf_op jit(solution)/shard_map/all_to_all | solution.py:67
  48.0 0.7 reshape.89
  48.7 0.1 copy.65
  48.8 28.3 %all-gather.2.cloned.1.call-done = bf16[16,256,256]{2,1,0:T(8,128)(2,1)} async-done(((bf16[16,64,256]{2,1,0:T(8,128)(2,1)}), bf16[16,256,256]{2,1,0:T(8,128)(2,1)}) %all-gather.2.cloned.1.call-update) | async-done | bytes 2097168 | tf_op jit(solution)/shard_map/all_gather | solution.py:73
  77.1 2.3 %convolution_convert_fusion = bf16[16,64,256]{2,1,0:T(8,128)(2,1)S(1)} fusion(bf16[16,64,256]{1,2,0:T(8,128)(2,1)S(1)} %bitcast.58, bf16[16,256,256]{2,1,0:T(8,128)(2,1)} %all-gather.2.cloned.1.call-done), kind=kOutput, calls=%fused_computation.28 | convolution fusion | flops 134479872 | bytes 3145728 | tf_op jit(solution)/shard_map/hik,hjk->hij/dot_general | solution.py:70
  79.5 1.0 copy.70
  80.4 0.7 reshape.92
  81.1 13.2 %all_to_all.47 = bf16[8,2,16384]{2,1,0:T(2,128)(2,1)S(1)} all-to-all(bf16[8,2,16384]{2,1,0:T(2,128)(2,1)S(1)} %reshape.92), channel_id=1, replica_groups=mesh['row'=4,'chan'=8] {'chan'}, dimensions={0} | all-to-all | bytes 1048576 | tf_op jit(solution)/shard_map/all_to_all | solution.py:77
  94.4 0.7 reshape.93
  95.0 0.3 fusion.51
  95.4 0.4 fusion.31
  95.8 0.2 copy.72
  96.1 0.4 copy-done.6
  96.5 0.4 fusion.3
  96.9 1.5 %copy.73 = bf16[128,64,32]{0,2,1:T(8,128)(2,1)S(1)} copy(bf16[128,64,32]{1,2,0:T(8,128)(2,1)S(1)} %fusion.3) | data formatting | bytes 1048576 | tf_op jit(solution)/shard_map/convert_element_type | solution.py:78
  98.5 0.3 fusion.32
  98.8 1.7 %fusion.18 = bf16[64,32,128]{2,1,0:T(8,128)(2,1)} fusion(f32[64,32,128]{2,1,0:T(8,128)S(1)} %fusion.32, bf16[128,128]{1,0:T(8,128)(2,1)S(1)} %copy-done.10, bf16[64,32,128]{2,1,0:T(8,128)(2,1)S(1)} %copy-done.1, f32[128]{0:T(128)S(1)} %copy-done.4, f32[128]{0:T(128)S(1)} %copy-done.5, f32[64,32]{1,0:T(8,128)S(1)} %copy.62, f32[64,32]{1,0:T(8,128)S(1)} %copy.60), kind=kOutput, calls=%fused_computation.27 | convolution fusion | flops 69992448 | bytes 2147328 | tf_op jit(solution)/shard_map/ijc,cd->ijd/dot_general | solution.py:82
  (30 shorter events, 0.4 us)
Async XLA Ops:
  6.5 3.2 %copy-start = (bf16[128,128]{1,0:T(8,128)(2,1)S(1)}, bf16[128,128]{1,0:T(8,128)(2,1)}, u32[]{:S(2)}) copy-start(bf16[128,128]{1,0:T(8,128)(2,1)} %param.19) | copy-start | bytes 98308
  6.5 5.0 %copy-start.1 = (bf16[64,32,128]{2,1,0:T(8,128)(2,1)S(1)}, bf16[64,32,128]{2,1,0:T(8,128)(2,1)}, u32[]{:S(2)}) copy-start(bf16[64,32,128]{2,1,0:T(8,128)(2,1)} %param.12) | copy-start | bytes 1572868
  6.5 5.0 %copy-start.4 = (f32[128]{0:T(128)S(1)}, f32[128]{0:T(128)}, u32[]{:S(2)}) copy-start(f32[128]{0:T(128)} %param.15) | copy-start | bytes 1540
  6.5 5.0 %copy-start.5 = (f32[128]{0:T(128)S(1)}, f32[128]{0:T(128)}, u32[]{:S(2)}) copy-start(f32[128]{0:T(128)} %param.14) | copy-start | bytes 1540
  6.5 5.0 %copy-start.8 = (bf16[128,128]{1,0:T(8,128)(2,1)S(1)}, bf16[128,128]{1,0:T(8,128)(2,1)}, u32[]{:S(2)}) copy-start(bf16[128,128]{1,0:T(8,128)(2,1)} %param.18) | copy-start | bytes 98308
  6.5 70.6 %all-gather.2.cloned.1.call-start = ((), (), s32[]{:S(2)}) async-start(), calls=%async_computation.3 | async-start | bytes 2621440 | tf_op jit(solution)/shard_map/all_gather | solution.py:73
  30.4 1.3 %copy-start.2 = (bf16[128,128]{1,0:T(8,128)(2,1)S(1)}, bf16[128,128]{1,0:T(8,128)(2,1)}, u32[]{:S(2)}) copy-start(bf16[128,128]{1,0:T(8,128)(2,1)} %param.17) | copy-start | bytes 98308
  30.5 1.9 %copy-start.9 = (bf16[128,128]{1,0:T(8,128)(2,1)S(1)}, bf16[128,128]{1,0:T(8,128)(2,1)}, u32[]{:S(2)}) copy-start(bf16[128,128]{1,0:T(8,128)(2,1)} %param.16) | copy-start | bytes 98308
  95.8 0.7 copy-start.6
  95.8 0.7 copy-start.7
  96.5 2.0 %copy-start.3 = (bf16[128,128]{1,0:T(8,128)(2,1)S(1)}, bf16[128,128]{1,0:T(8,128)(2,1)}, u32[]{:S(2)}) copy-start(bf16[128,128]{1,0:T(8,128)(2,1)} %param.23) | copy-start | bytes 98308
  96.9 1.9 %copy-start.10 = (bf16[128,128]{1,0:T(8,128)(2,1)S(1)}, bf16[128,128]{1,0:T(8,128)(2,1)}, u32[]{:S(2)}) copy-start(bf16[128,128]{1,0:T(8,128)(2,1)} %param.22) | copy-start | bytes 98308
Sparse Core Ops, SparseCore 0:
  31.8 45.2 all-gather.1
where the time goes:
time: 108 us; the launch traced here: 107 us
  blocking collectives  40.1 us (37%)
  waiting for transfers between devices  28.4 us (26%)
  between operations  13.7 us (13%)
  local copies, waits for them, and re-layouts  12.3 us (11%)
  matrix products  9.94 us (9%)
  other arithmetic  2.96 us (3%)
    all_gather x1, waiting for transfers between devices, local(): lax.all_gather(right_x, 'row', axis=1, tiled=True)  28.3 us
    all_to_all x1, blocking collectives, local(): lax.all_to_all(right, 'chan', split_axis=0, concat_axis=2, tiled=True)  14.7 us
    all_to_all x1, blocking collectives, local(): lax.all_to_all(crossed_b, 'chan', split_axis=2, concat_axis=0, tiled=True)  13.2 us
    all_to_all x1, blocking collectives, local(): lax.all_to_all(left, 'chan', split_axis=0, concat_axis=2, tiled=True)  12.2 us
    unnamed x28, local copies, waits for them, and re-layouts  4.5 us
    convert_element_type x2, local copies, waits for them, and re-layouts, edges(): (pair_mask[None] * jax.nn.sigmoid(gate_pre) * proj_pre).astype(jnp.bfloat16)  3.39 us
    dot_general x2, matrix products, edges(): jnp.einsum('ijc,ch->hij', normed, proj_w, preferred_element_type=jnp.floa...  2.52 us
    dot_general x1, matrix products, local(): jnp.einsum('hik,hjk->hij', left_x, lax.all_gather(right_x, 'row', axis=1,...  2.35 us
  transfers between devices with their start and end apart: 1, of which 1 were waited for; matrix products, arithmetic and copies ran while one was open for 5% of the time, Pallas kernels for 0%

commit v1 on v0

v1 whole, which is shorter than its diff:
```python
import functools
import math

import jax
import jax.numpy as jnp
from jax import lax
from jax.experimental import pallas as pl
from jax.experimental.pallas import tpu as pltpu
from jax.sharding import PartitionSpec as P

MESH = pl.DeviceIdType.MESH
F32 = jnp.float32
BF16 = jnp.bfloat16
epsilon = 1e-05


def contract(a, b, da, db):
    return lax.dot_general(a, b, (((da,), (db,)), ((), ())), preferred_element_type=F32)


def column(row_ref):
    width = row_ref.shape[1]
    return jnp.transpose(jnp.broadcast_to(row_ref[...], (width, width)))


def kernel(
    nr, nc, parts,
    pair, tile_mask, in_gain, in_shift, left_gate, left_proj, right_gate, right_proj,
    out_gain, out_shift, out_gate, out_proj,
    updated,
    normed, stage, gates, mask, left_w, right_w, means, scales,
    left_send, right_send, left_all, right_all, cross_send, cross_all,
    ls, lr, rs, rr, xs, xr, zs, zr,
):
    rows, cols, width = pair.shape
    half = width // 2
    mine = half // nc
    each = mine // parts
    tiles = tile_mask.shape[0]
    tile = rows * nr // tiles
    r = lax.axis_index("row")
    c = lax.axis_index("chan")

    barrier = pltpu.get_barrier_semaphore()

    @pl.loop(1, nc)
    def _(d):
        pl.semaphore_signal(
            barrier, inc=1, device_id={"chan": lax.rem(c + d, nc)}, device_id_type=MESH
        )

    @pl.when(r > 0)
    def _():
        pl.semaphore_signal(barrier, inc=1, device_id={"row": r - 1}, device_id_type=MESH)

    @pl.when(r < nr - 1)
    def _():
        pl.semaphore_signal(barrier, inc=1, device_id={"row": r + 1}, device_id_type=MESH)

    group = 8

    @pl.loop(0, rows // group)
    def _(g):
        v = pair[pl.ds(g * group, group)].astype(F32).reshape(group * cols, width)
        m = jnp.mean(v, axis=1, keepdims=True)
        s = jnp.mean(v * v, axis=1, keepdims=True)
        n = (v - m) * lax.rsqrt(s - m * m + epsilon) * in_gain[...] + in_shift[...]
        normed[pl.ds(pl.multiple_of(g * group * cols, group * cols), group * cols), :] = (
            n.astype(BF16).astype(F32)
        )

    tm = tile_mask[...].astype(F32)
    ids = lax.broadcasted_iota(jnp.int32, (cols, tiles), 0) + c * cols
    low = lax.broadcasted_iota(jnp.int32, (cols, tiles), 1) * tile
    col_hot = jnp.where((ids >= low) & (ids < low + tile), 1.0, 0.0)
    lane_t = lax.broadcasted_iota(jnp.int32, (tiles, width), 1)
    ids = jnp.where(lane_t < half, lane_t, lane_t - half) + r * rows
    low = lax.broadcasted_iota(jnp.int32, (tiles, width), 0) * tile
    row_hot = jnp.where((ids >= low) & (ids < low + tile), 1.0, 0.0)
    mask[...] = contract(contract(col_hot, tm, 1, 1), row_hot, 1, 0)

    def paired(w_ref):
        t = jnp.transpose(w_ref[...].astype(F32))
        return jnp.concatenate([t[:half], t[half:]], axis=1).astype(BF16)

    right_w[:half] = paired(right_gate)
    right_w[half:] = paired(right_proj)
    left_w[:half] = paired(left_gate)
    left_w[half:] = paired(left_proj)

    def at_column(k):
        return normed[pl.ds(k, rows, stride=cols), :].astype(BF16)

    def edges(w_ref, send):
        w = w_ref[...]
        empty = jnp.zeros((rows, width), BF16)

        @pl.loop(0, cols, unroll=4)
        def _(k):
            n = at_column(k)
            both = jnp.concatenate(
                [jnp.concatenate([n, empty], axis=1), jnp.concatenate([empty, n], axis=1)], axis=0
            )
            pre = contract(w, both, 1, 1)
            edge = mask[pl.ds(k, 1), :] * jax.nn.sigmoid(pre[:half]) * pre[half:]
            stage[pl.ds(k, half, stride=cols), :] = edge

        @pl.loop(0, half // group)
        def _(g):
            at = pl.ds(pl.multiple_of(g * group * cols, group * cols), group * cols)
            send[pl.ds(g * group, group)] = stage[at, :].astype(BF16).reshape(group, cols, width)

    def part_of(q):
        return pl.ds(q * each, each)

    def right_copy(d, q):
        to = lax.rem(c + d, nc)
        return pltpu.make_async_remote_copy(
            src_ref=right_send.at[pl.ds(to * mine + q * each, each)],
            dst_ref=right_all.at[r, part_of(q), pl.ds(pl.multiple_of(c * cols, cols), cols), :],
            send_sem=rs.at[d, q], recv_sem=rr.at[d, q],
            device_id={"chan": to}, device_id_type=MESH,
        )

    def left_copy(d, q):
        to = lax.rem(c + d, nc)
        return pltpu.make_async_remote_copy(
            src_ref=left_send.at[pl.ds(to * mine + q * each, each)],
            dst_ref=left_all.at[part_of(q), pl.ds(pl.multiple_of(c * cols, cols), cols), :],
            send_sem=ls.at[d, q], recv_sem=lr.at[d, q],
            device_id={"chan": to}, device_id_type=MESH,
        )

    def cross_copy(d, q):
        to = lax.rem(c + d, nc)
        return pltpu.make_async_remote_copy(
            src_ref=cross_send.at[part_of(q), pl.ds(pl.multiple_of(to * cols, cols), cols), :],
            dst_ref=cross_all.at[pl.ds(c * mine + q * each, each)],
            send_sem=xs.at[d, q], recv_sem=xr.at[d, q],
            device_id={"chan": to}, device_id_type=MESH,
        )

    def row_copy(block, q, way):
        return pltpu.make_async_remote_copy(
            src_ref=right_all.at[block, part_of(q)],
            dst_ref=right_all.at[block, part_of(q)],
            send_sem=zs.at[way, block, q], recv_sem=zr.at[block, q],
            device_id={"row": r + 1 - 2 * way}, device_id_type=MESH,
        )

    def each_peer(act):
        @pl.loop(1, nc)
        def _(d):
            act(d)

    own_cols = pl.ds(pl.multiple_of(c * cols, cols), cols)

    edges(right_w, right_send)
    pl.semaphore_wait(
        barrier, nc - 1 + jnp.where(r > 0, 1, 0) + jnp.where(r < nr - 1, 1, 0)
    )
    for q in range(parts):
        each_peer(lambda d: right_copy(d, q).start())
    right_all[r, :, own_cols, :] = right_send[pl.ds(c * mine, mine)]

    edges(left_w, left_send)
    for q in range(parts):
        each_peer(lambda d: left_copy(d, q).start())
    left_all[:, own_cols, :] = left_send[pl.ds(c * mine, mine)]

    lane = lax.broadcasted_iota(jnp.int32, (rows, width), 1)

    def products(q):
        each_peer(lambda d: left_copy(d, q).wait_recv())

        @pl.loop(0, nr)
        def _(b):
            for h in range(q * each, (q + 1) * each):
                both = contract(right_all[b, h], left_all[h], 0, 0)
                x = jnp.where(lane < half, both[:half], both[half:]).astype(BF16)
                cross_send[h, pl.ds(pl.multiple_of(b * rows, rows), rows), :] = x

        each_peer(lambda d: cross_copy(d, q).start())
        cross_all[pl.ds(c * mine + q * each, each)] = cross_send[part_of(q), own_cols, :]

    def pass_on(block, q, way, arrives):
        there = (block >= 0) & (block < nr)

        @pl.when(there)
        def _():
            if arrives:
                row_copy(block, q, way).wait_recv()

            @pl.when((r < nr - 1) if way == 0 else (r > 0))
            def _():
                row_copy(block, q, way).start()

    for t in range(parts + nr - 1):
        if t < parts:
            each_peer(lambda d: right_copy(d, t).wait_recv())
        for s in range(nr):
            q = t - s
            if 0 <= q < parts:
                pass_on(r - s, q, 0, s > 0)
                pass_on(r + s, q, 1, s > 0)
        if t == 0:
            @pl.loop(0, cols, unroll=4)
            def _(k):
                gates[k] = jax.nn.sigmoid(contract(at_column(k), out_gate[...], 1, 0))

        if t >= nr - 1:
            products(t - (nr - 1))

    for q in range(parts):
        each_peer(lambda d: cross_copy(d, q).wait_recv())

    def add_up(h, sums):
        x = cross_all[h].astype(F32)
        stage[pl.ds(pl.multiple_of(h * cols, cols), cols), :] = x
        return sums[0] + x, sums[1] + x * x

    zero = jnp.zeros((cols, width), F32)
    total, squares = lax.fori_loop(0, half, add_up, (zero, zero), unroll=4)
    total = total + pltpu.roll(total, half, 1)
    squares = squares + pltpu.roll(squares, half, 1)
    m = total / width
    means[...] = m
    scales[...] = lax.rsqrt(squares / width - m * m + epsilon)

    lane_h = lax.broadcasted_iota(jnp.int32, (half, width), 1)
    g = column(out_gain)
    s = column(out_shift)
    gain = jnp.where(lane_h < half, g[:half], g[half:])
    shift = jnp.where(lane_h < half, s[:half], s[half:])
    w_out = jnp.concatenate([out_proj[:half], out_proj[half:]], axis=1)

    @pl.loop(0, cols, unroll=4)
    def _(j):
        x = stage[pl.ds(j, half, stride=cols), :]
        x = (x - means[pl.ds(j, 1), :]) * scales[pl.ds(j, 1), :] * gain + shift
        y = contract(x.astype(BF16), w_out, 0, 0)
        normed[pl.ds(j, rows, stride=cols), :] = gates[j] * (y[:half, :width] + y[half:, width:])

    @pl.loop(0, rows // group)
    def _(g):
        at = pl.ds(pl.multiple_of(g * group * cols, group * cols), group * cols)
        updated[pl.ds(g * group, group)] = normed[at, :].astype(BF16).reshape(group, cols, width)

    for q in range(parts):
        def sent(d):
            right_copy(d, q).wait_send()
            left_copy(d, q).wait_send()
            cross_copy(d, q).wait_send()

        each_peer(sent)

    @pl.loop(0, nr)
    def _(block):
        for q in range(parts):
            @pl.when((block <= r) & (r < nr - 1))
            def _():
                row_copy(block, q, 0).wait_send()

            @pl.when((block >= r) & (r > 0))
            def _():
                row_copy(block, q, 1).wait_send()


def local(nr, nc, pair, tile_mask, in_gain, in_shift, left_gate, left_proj, right_gate, right_proj,
          out_gain, out_shift, out_gate, out_proj):
    rows, cols, width = pair.shape
    half = width // 2
    assert rows == half
    mine = half // nc
    parts = math.gcd(mine, 4)
    total = cols * nc
    dma = pltpu.SemaphoreType.DMA
    vmem = pltpu.VMEM
    return pl.pallas_call(
        functools.partial(kernel, nr, nc, parts),
        out_shape=jax.ShapeDtypeStruct(pair.shape, BF16),
        in_specs=[pl.BlockSpec(memory_space=pltpu.VMEM)] * 12,
        out_specs=pl.BlockSpec(memory_space=pltpu.VMEM),
        scratch_shapes=[
            vmem((rows * cols, width), F32),
            vmem((half * cols, width), F32),
            vmem((cols, rows, width), F32),
            vmem((cols, width), F32),
            vmem((width, 2 * width), BF16),
            vmem((width, 2 * width), BF16),
            vmem((cols, width), F32),
            vmem((cols, width), F32),
            vmem((half, cols, width), BF16),
            vmem((half, cols, width), BF16),
            vmem((mine, total, width), BF16),
            vmem((nr, mine, total, width), BF16),
            vmem((mine, rows * nr, width), BF16),
            vmem((half, cols, width), BF16),
            dma((nc, parts)), dma((nc, parts)),
            dma((nc, parts)), dma((nc, parts)),
            dma((nc, parts)), dma((nc, parts)),
            dma((2, nr, parts)), dma((nr, parts)),
        ],
        compiler_params=pltpu.CompilerParams(
            collective_id=0, has_side_effects=True, vmem_limit_bytes=48 * 1024 * 1024
        ),
    )(
        pair, tile_mask, in_gain[None], in_shift[None], left_gate, left_proj, right_gate,
        right_proj, out_gain[None], out_shift[None], out_gate, out_proj,
    )


def solution(mesh):
    placed = (P("row", "chan", None), P(), P(), P(), P(), P(), P(), P(), P(), P(), P(), P())
    return jax.shard_map(
        functools.partial(local, mesh.shape["row"], mesh.shape["chan"]),
        mesh=mesh, in_specs=placed, out_specs=P("row", "chan", None), check_vma=False,
    )
```

time: 108 us -> 65.1 us (0.60)
  Pallas kernels: 0 us -> 56.6 us
  blocking collectives: 40.1 us -> 0 us
  waiting for transfers between devices: 28.4 us -> 0 us
  between operations: 13.7 us -> 0.02 us
  matrix products: 9.94 us -> 0 us
  local copies, waits for them, and re-layouts: 12.3 us -> 7.84 us
  other arithmetic: 2.96 us -> 0 us
    pallas_call x0 -> x1, Pallas kernels: none -> 56.6 us  [local(): pl.pallas_call(functools.partial(kernel, nr, nc, parts), out_shape=jax.Sh...]
    all_to_all x3 -> x0, blocking collectives: 40.1 us -> none  [the longest x1 14.7 us: local(): lax.all_to_all(right, 'chan', split_axis=0, concat_axis=2, tiled=True)]
    all_gather x1 -> x0, waiting for transfers between devices: 28.3 us -> none  [local(): lax.all_gather(right_x, 'row', axis=1, tiled=True)]
    dot_general x8 -> x0, matrix products: 9.94 us -> none  [the longest x2 2.52 us: edges(): jnp.einsum('ijc,ch->hij', normed, proj_w, preferred_element_type=jnp.floa...]
    convert_element_type x5 -> x0, local copies, waits for them, and re-layouts: 6.13 us -> none  [the longest x2 3.39 us: edges(): (pair_mask[None] * jax.nn.sigmoid(gate_pre) * proj_pre).astype(jnp.bfloat16)]
    unnamed x28 -> x25, local copies, waits for them, and re-layouts: 4.5 us -> 7.84 us
    reduce_sum x2 -> x0, other arithmetic: 2.15 us -> none  [the longest x1 1.72 us: norm_last(): average = jnp.mean(values, axis=-1, keepdims=True)]
    all_to_all x3 -> x0, local copies, waits for them, and re-layouts: 1.34 us -> none  [the longest x2 1.23 us: local(): lax.all_to_all(right, 'chan', split_axis=0, concat_axis=2, tiled=True)]
  transfers between devices with their start and end apart: 1 -> 0, of which waited for: 1 -> 0; matrix products, arithmetic and copies ran while one was open for 5% -> 0% of each run, Pallas kernels for 0% -> 0%
where the time goes in v1:
time: 65.1 us; the launch traced here: 64.4 us
  Pallas kernels  56.6 us (87%)
  local copies, waits for them, and re-layouts  7.84 us (12%)
    pallas_call x1, Pallas kernels, local(): pl.pallas_call(functools.partial(kernel, nr, nc, parts), out_shape=jax.Sh...  56.6 us
    unnamed x25, local copies, waits for them, and re-layouts  7.84 us

profile of v1, /device:TPU:0, one launch (start us, length us, event | category | flops | bytes accessed | tf_op | source)
XLA Modules:
  0.0 64.4 jit_solution(8131036348870950980)
XLA Ops:
  0.0 0.0 copy-start.11
  0.0 0.0 copy-start.8
  0.0 0.0 copy-start.9
  0.0 0.0 copy-start.10
  0.0 0.6 %copy-done.11 = f32[128]{0:T(128)S(1)} copy-done((f32[128]{0:T(128)S(1)}, f32[128]{0:T(128)}, u32[]{:S(2)}) %copy-start.11) | copy-done | bytes 536
  0.7 0.0 copy-done.8
  0.7 0.0 copy-done.9
  0.7 0.0 copy-done.10
  0.7 0.0 copy-start
  0.7 1.0 %copy-done = bf16[64,32,128]{2,1,0:T(8,128)(2,1)S(1)} copy-done((bf16[64,32,128]{2,1,0:T(8,128)(2,1)S(1)}, bf16[64,32,128]{2,1,0:T(8,128)(2,1)}, u32[]{:S(2)}) %copy-start) | copy-done | bytes 524312
  1.7 0.0 copy-start.1
  1.7 0.8 %copy-done.1 = s32[64,64]{1,0:T(8,128)S(1)} copy-done((s32[64,64]{1,0:T(8,128)S(1)}, s32[64,64]{1,0:T(8,128)}, u32[]{:S(2)}) %copy-start.1) | copy-done | bytes 16408
  2.5 0.0 copy-start.2
  2.5 0.8 %copy-done.2 = bf16[128,128]{1,0:T(8,128)(2,1)S(1)} copy-done((bf16[128,128]{1,0:T(8,128)(2,1)S(1)}, bf16[128,128]{1,0:T(8,128)(2,1)}, u32[]{:S(2)}) %copy-start.2) | copy-done | bytes 32792
  3.3 0.0 copy-start.3
  3.3 0.8 %copy-done.3 = bf16[128,128]{1,0:T(8,128)(2,1)S(1)} copy-done((bf16[128,128]{1,0:T(8,128)(2,1)S(1)}, bf16[128,128]{1,0:T(8,128)(2,1)}, u32[]{:S(2)}) %copy-start.3) | copy-done | bytes 32792
  4.0 0.0 copy-start.4
  4.0 0.8 %copy-done.4 = bf16[128,128]{1,0:T(8,128)(2,1)S(1)} copy-done((bf16[128,128]{1,0:T(8,128)(2,1)S(1)}, bf16[128,128]{1,0:T(8,128)(2,1)}, u32[]{:S(2)}) %copy-start.4) | copy-done | bytes 32792
  4.8 0.0 copy-start.5
  4.8 0.8 %copy-done.5 = bf16[128,128]{1,0:T(8,128)(2,1)S(1)} copy-done((bf16[128,128]{1,0:T(8,128)(2,1)S(1)}, bf16[128,128]{1,0:T(8,128)(2,1)}, u32[]{:S(2)}) %copy-start.5) | copy-done | bytes 32792
  5.5 0.0 copy-start.6
  5.5 0.8 %copy-done.6 = bf16[128,128]{1,0:T(8,128)(2,1)S(1)} copy-done((bf16[128,128]{1,0:T(8,128)(2,1)S(1)}, bf16[128,128]{1,0:T(8,128)(2,1)}, u32[]{:S(2)}) %copy-start.6) | copy-done | bytes 32792
  6.3 0.0 copy-start.7
  6.3 0.8 %copy-done.7 = bf16[128,128]{1,0:T(8,128)(2,1)S(1)} copy-done((bf16[128,128]{1,0:T(8,128)(2,1)S(1)}, bf16[128,128]{1,0:T(8,128)(2,1)}, u32[]{:S(2)}) %copy-start.7) | copy-done | bytes 32792
  7.1 56.6 %shard_map.118 = bf16[64,32,128]{2,1,0:T(8,128)(2,1)S(1)} custom-call(bf16[64,32,128]{2,1,0:T(8,128)(2,1)S(1)} %copy-done, s32[64,64]{1,0:T(8,128)S(1)} %copy-done.1, f32[1,128]{1,0:T(1,128)S(1)} %bitcast.4, f32[1,128]{1,0:T(1,128)S(1)} %bitcast.5, bf16[128,128]{1,0:T(8,128)(2,1)S(1)} %copy-done.2, bf16[128,128]{1,0:T(8,128)(2,1)S(1)} %copy-done.3, ...), custom_call_target="tpu_custom_call" | custom-call | tf_op jit(solution)/shard_map/pallas_call | solution.py:279
  63.6 0.8 %copy.14 = bf16[64,32,128]{2,1,0:T(8,128)(2,1)} copy(bf16[64,32,128]{2,1,0:T(8,128)(2,1)S(1)} %shard_map.118) | data formatting | bytes 1048576
Async XLA Ops:
  0.0 0.7 %copy-start.11 = (f32[128]{0:T(128)S(1)}, f32[128]{0:T(128)}, u32[]{:S(2)}) copy-start(f32[128]{0:T(128)} %param.21) | copy-start | bytes 1540
  0.0 0.7 %copy-start.8 = (f32[128]{0:T(128)S(1)}, f32[128]{0:T(128)}, u32[]{:S(2)}) copy-start(f32[128]{0:T(128)} %param.14) | copy-start | bytes 1540
  0.0 0.7 %copy-start.9 = (f32[128]{0:T(128)S(1)}, f32[128]{0:T(128)}, u32[]{:S(2)}) copy-start(f32[128]{0:T(128)} %param.15) | copy-start | bytes 1540
  0.0 0.7 %copy-start.10 = (f32[128]{0:T(128)S(1)}, f32[128]{0:T(128)}, u32[]{:S(2)}) copy-start(f32[128]{0:T(128)} %param.20) | copy-start | bytes 1540
  0.7 1.0 %copy-start = (bf16[64,32,128]{2,1,0:T(8,128)(2,1)S(1)}, bf16[64,32,128]{2,1,0:T(8,128)(2,1)}, u32[]{:S(2)}) copy-start(bf16[64,32,128]{2,1,0:T(8,128)(2,1)} %pair.1) | copy-start | bytes 1572868
  1.7 0.8 %copy-start.1 = (s32[64,64]{1,0:T(8,128)S(1)}, s32[64,64]{1,0:T(8,128)}, u32[]{:S(2)}) copy-start(s32[64,64]{1,0:T(8,128)} %tile_mask.1) | copy-start | bytes 49156
  2.5 0.8 %copy-start.2 = (bf16[128,128]{1,0:T(8,128)(2,1)S(1)}, bf16[128,128]{1,0:T(8,128)(2,1)}, u32[]{:S(2)}) copy-start(bf16[128,128]{1,0:T(8,128)(2,1)} %left_gate.1) | copy-start | bytes 98308
  3.3 0.8 %copy-start.3 = (bf16[128,128]{1,0:T(8,128)(2,1)S(1)}, bf16[128,128]{1,0:T(8,128)(2,1)}, u32[]{:S(2)}) copy-start(bf16[128,128]{1,0:T(8,128)(2,1)} %left_proj.1) | copy-start | bytes 98308
  4.0 0.8 %copy-start.4 = (bf16[128,128]{1,0:T(8,128)(2,1)S(1)}, bf16[128,128]{1,0:T(8,128)(2,1)}, u32[]{:S(2)}) copy-start(bf16[128,128]{1,0:T(8,128)(2,1)} %right_gate.1) | copy-start | bytes 98308
  4.8 0.8 %copy-start.5 = (bf16[128,128]{1,0:T(8,128)(2,1)S(1)}, bf16[128,128]{1,0:T(8,128)(2,1)}, u32[]{:S(2)}) copy-start(bf16[128,128]{1,0:T(8,128)(2,1)} %right_proj.1) | copy-start | bytes 98308
  5.5 0.8 %copy-start.6 = (bf16[128,128]{1,0:T(8,128)(2,1)S(1)}, bf16[128,128]{1,0:T(8,128)(2,1)}, u32[]{:S(2)}) copy-start(bf16[128,128]{1,0:T(8,128)(2,1)} %out_gate.1) | copy-start | bytes 98308
  6.3 0.8 %copy-start.7 = (bf16[128,128]{1,0:T(8,128)(2,1)S(1)}, bf16[128,128]{1,0:T(8,128)(2,1)}, u32[]{:S(2)}) copy-start(bf16[128,128]{1,0:T(8,128)(2,1)} %out_proj.1) | copy-start | bytes 98308

commit v2 on v1

--- a/solution.py
+++ b/solution.py
@@ -25,13 +25,27 @@
 
 def kernel(
     nr, nc, parts,
-    pair, tile_mask, in_gain, in_shift, left_gate, left_proj, right_gate, right_proj,
-    out_gain, out_shift, out_gate, out_proj,
-    updated,
-    normed, stage, gates, mask, left_w, right_w, means, scales,
+    *refs,
+):
+    operands, (updated,), held, rest = refs[:12], refs[12:13], refs[13:25], refs[25:]
+    body(nr, nc, parts, operands, held, updated, *rest)
+
+
+def body(
+    nr, nc, parts, operands, held, updated,
+    fetched, normed, stage, gates, mask, left_w, right_w, means, scales,
     left_send, right_send, left_all, right_all, cross_send, cross_all,
-    ls, lr, rs, rr, xs, xr, zs, zr,
+    left_far, far_send,
+    ls, lr, rs, rr, xs, xr, zs, zr, fs, fr, gs, gr,
 ):
+    fetches = [
+        pltpu.make_async_copy(source, target, fetched.at[n])
+        for n, (source, target) in enumerate(zip(operands, held))
+    ]
+    for fetch in fetches:
+        fetch.start()
+    (pair, tile_mask, in_gain, in_shift, left_gate, left_proj, right_gate, right_proj,
+     out_gain, out_shift, out_gate, out_proj) = held
     rows, cols, width = pair.shape
     half = width // 2
     mine = half // nc
@@ -57,6 +71,9 @@
     def _():
         pl.semaphore_signal(barrier, inc=1, device_id={"row": r + 1}, device_id_type=MESH)
 
+    for n in (0, 2, 3):
+        fetches[n].wait()
+
     group = 8
 
     @pl.loop(0, rows // group)
@@ -68,6 +85,9 @@
         normed[pl.ds(pl.multiple_of(g * group * cols, group * cols), group * cols), :] = (
             n.astype(BF16).astype(F32)
         )
+
+    for n in (1, 4, 5, 6, 7, 8, 9, 10, 11):
+        fetches[n].wait()
 
     tm = tile_mask[...].astype(F32)
     ids = lax.broadcasted_iota(jnp.int32, (cols, tiles), 0) + c * cols
@@ -170,46 +190,143 @@
 
     lane = lax.broadcasted_iota(jnp.int32, (rows, width), 1)
 
-    def products(q):
-        each_peer(lambda d: left_copy(d, q).wait_recv())
-
-        @pl.loop(0, nr)
+    first, last = r == 0, r == nr - 1
+    share = nr // 2
+    low_part, high_part = pl.ds(0, share * rows), pl.ds(share * rows, (nr - share) * rows)
+
+    def left_over(q, way):
+        return pltpu.make_async_remote_copy(
+            src_ref=left_all.at[part_of(q)], dst_ref=left_far.at[part_of(q)],
+            send_sem=fs.at[q], recv_sem=fr.at[q],
+            device_id={"row": r + 1 - 2 * way}, device_id_type=MESH,
+        )
+
+    def products_over(q, way):
+        there = high_part if way else low_part
+        return pltpu.make_async_remote_copy(
+            src_ref=far_send.at[part_of(q), there], dst_ref=cross_send.at[part_of(q), there],
+            send_sem=gs.at[q], recv_sem=gr.at[q],
+            device_id={"row": r + 1 - 2 * way}, device_id_type=MESH,
+        )
+
+    def multiply(q, start, stop, left, into):
+        @pl.loop(start, stop)
         def _(b):
             for h in range(q * each, (q + 1) * each):
-                both = contract(right_all[b, h], left_all[h], 0, 0)
+                both = contract(right_all[b, h], left[h], 0, 0)
                 x = jnp.where(lane < half, both[:half], both[half:]).astype(BF16)
-                cross_send[h, pl.ds(pl.multiple_of(b * rows, rows), rows), :] = x
-
+                into[h, pl.ds(pl.multiple_of(b * rows, rows), rows), :] = x
+
+    def send_products(q):
         each_peer(lambda d: cross_copy(d, q).start())
         cross_all[pl.ds(c * mine + q * each, each)] = cross_send[part_of(q), own_cols, :]
 
+    def own_products(q):
+        @pl.when(first)
+        def _():
+            multiply(q, 0, share, left_all, cross_send)
+
+        @pl.when(last)
+        def _():
+            multiply(q, share, nr, left_all, cross_send)
+
+        @pl.when(jnp.logical_not(first | last))
+        def _():
+            each_peer(lambda d: left_copy(d, q).wait_recv())
+            multiply(q, 0, nr, left_all, cross_send)
+            send_products(q)
+
+    def far_products(q):
+        @pl.when(r == 1)
+        def _():
+            left_over(q, 0).wait_recv()
+            multiply(q, share, nr, left_far, far_send)
+            products_over(q, 1).start()
+
+        @pl.when(r == nr - 2)
+        def _():
+            left_over(q, 1).wait_recv()
+            multiply(q, 0, share, left_far, far_send)
+            products_over(q, 0).start()
+
+        @pl.when(first)
+        def _():
+            products_over(q, 1).wait_recv()
+            send_products(q)
+
+        @pl.when(last)
+        def _():
+            products_over(q, 0).wait_recv()
+            send_products(q)
+
     def pass_on(block, q, way, arrives):
-        there = (block >= 0) & (block < nr)
+        if way == 0:
+            there = (block >= 0) & jnp.logical_not(last & (block < share))
+            goes = (r < nr - 2) | ((r == nr - 2) & (block >= share))
+        else:
+            there = (block < nr) & jnp.logical_not(first & (block >= share))
+            goes = (r > 1) | ((r == 1) & (block < share))
 
         @pl.when(there)
         def _():
             if arrives:
                 row_copy(block, q, way).wait_recv()
 
-            @pl.when((r < nr - 1) if way == 0 else (r > 0))
+            @pl.when(goes)
             def _():
                 row_copy(block, q, way).start()
+
+    @pl.when(first | last)
+    def _():
+        def right_on(q):
+            each_peer(lambda d: right_copy(d, q).wait_recv())
+
+            @pl.when(first)
+            def _():
+                row_copy(r, q, 0).start()
+
+            @pl.when(last)
+            def _():
+                row_copy(r, q, 1).start()
+
+        def left_on(q):
+            each_peer(lambda d: left_copy(d, q).wait_recv())
+
+            @pl.when(first)
+            def _():
+                left_over(q, 0).start()
+
+            @pl.when(last)
+            def _():
+                left_over(q, 1).start()
+
+        for q in range(parts + 1):
+            if q < parts:
+                right_on(q)
+            if q > 0:
+                left_on(q - 1)
 
     for t in range(parts + nr - 1):
         if t < parts:
-            each_peer(lambda d: right_copy(d, t).wait_recv())
-        for s in range(nr):
+            @pl.when(jnp.logical_not(first | last))
+            def _():
+                each_peer(lambda d: right_copy(d, t).wait_recv())
+                pass_on(r, t, 0, False)
+                pass_on(r, t, 1, False)
+        for s in range(1, nr - 1):
             q = t - s
             if 0 <= q < parts:
-                pass_on(r - s, q, 0, s > 0)
-                pass_on(r + s, q, 1, s > 0)
+                pass_on(r - s, q, 0, True)
+                pass_on(r + s, q, 1, True)
         if t == 0:
             @pl.loop(0, cols, unroll=4)
             def _(k):
                 gates[k] = jax.nn.sigmoid(contract(at_column(k), out_gate[...], 1, 0))
 
+        if 0 <= t - (nr - 2) < parts:
+            own_products(t - (nr - 2))
         if t >= nr - 1:
-            products(t - (nr - 1))
+            far_products(t - (nr - 1))
 
     for q in range(parts):
         each_peer(lambda d: cross_copy(d, q).wait_recv())
@@ -254,14 +371,22 @@
 
         each_peer(sent)
 
-    @pl.loop(0, nr)
-    def _(block):
-        for q in range(parts):
-            @pl.when((block <= r) & (r < nr - 1))
+    for q in range(parts):
+        @pl.when(first | last)
+        def _():
+            left_over(q, 0).wait_send()
+
+        @pl.when((r == 1) | (r == nr - 2))
+        def _():
+            products_over(q, 0).wait_send()
+
+        @pl.loop(0, nr)
+        def _(block):
+            @pl.when((block <= r) & ((r < nr - 2) | ((r == nr - 2) & (block >= share))))
             def _():
                 row_copy(block, q, 0).wait_send()
 
-            @pl.when((block >= r) & (r > 0))
+            @pl.when((block >= r) & ((r > 1) | ((r == 1) & (block < share))))
             def _():
                 row_copy(block, q, 1).wait_send()
 
@@ -270,18 +395,23 @@
           out_gain, out_shift, out_gate, out_proj):
     rows, cols, width = pair.shape
     half = width // 2
-    assert rows == half
+    assert rows == half and nr >= 4 and nr % 2 == 0
     mine = half // nc
     parts = math.gcd(mine, 4)
     total = cols * nc
     dma = pltpu.SemaphoreType.DMA
     vmem = pltpu.VMEM
+    operands = (
+        pair, tile_mask, in_gain[None], in_shift[None], left_gate, left_proj, right_gate,
+        right_proj, out_gain[None], out_shift[None], out_gate, out_proj,
+    )
     return pl.pallas_call(
         functools.partial(kernel, nr, nc, parts),
         out_shape=jax.ShapeDtypeStruct(pair.shape, BF16),
-        in_specs=[pl.BlockSpec(memory_space=pltpu.VMEM)] * 12,
+        in_specs=[pl.BlockSpec(memory_space=pl.ANY)] * 12,
         out_specs=pl.BlockSpec(memory_space=pltpu.VMEM),
-        scratch_shapes=[
+        scratch_shapes=[vmem(a.shape, a.dtype) for a in operands] + [
+            dma((len(operands),)),
             vmem((rows * cols, width), F32),
             vmem((half * cols, width), F32),
             vmem((cols, rows, width), F32),
@@ -296,18 +426,18 @@
             vmem((nr, mine, total, width), BF16),
             vmem((mine, rows * nr, width), BF16),
             vmem((half, cols, width), BF16),
+            vmem((mine, total, width), BF16),
+            vmem((mine, rows * nr, width), BF16),
             dma((nc, parts)), dma((nc, parts)),
             dma((nc, parts)), dma((nc, parts)),
             dma((nc, parts)), dma((nc, parts)),
             dma((2, nr, parts)), dma((nr, parts)),
+            dma((parts,)), dma((parts,)), dma((parts,)), dma((parts,)),
         ],
         compiler_params=pltpu.CompilerParams(
-            collective_id=0, has_side_effects=True, vmem_limit_bytes=48 * 1024 * 1024
+            collective_id=0, has_side_effects=True, vmem_limit_bytes=60 * 1024 * 1024
         ),
-    )(
-        pair, tile_mask, in_gain[None], in_shift[None], left_gate, left_proj, right_gate,
-        right_proj, out_gain[None], out_shift[None], out_gate, out_proj,
-    )
+    )(*operands)
 
 
 def solution(mesh):

time: 65.1 us -> 55 us (0.84)
  local copies, waits for them, and re-layouts: 7.84 us -> 1.87 us
  Pallas kernels: 56.6 us -> 53 us
    unnamed x25 -> x1, local copies, waits for them, and re-layouts: 7.84 us -> 1.87 us
    pallas_call x1, Pallas kernels: 56.6 us -> 53 us  [local(): pl.pallas_call(functools.partial(kernel, nr, nc, parts), out_shape=jax.Sh...]
where the time goes in v2:
time: 55 us; the launch traced here: 54.9 us
  Pallas kernels  53 us (96%)
  local copies, waits for them, and re-layouts  1.87 us (3%)
    pallas_call x1, Pallas kernels, local(): pl.pallas_call(functools.partial(kernel, nr, nc, parts), out_shape=jax.Sh...  53 us
    unnamed x1, local copies, waits for them, and re-layouts  1.87 us

profile of v2, /device:TPU:0, one launch (start us, length us, event | category | flops | bytes accessed | tf_op | source)
XLA Modules:
  0.0 54.9 jit_solution(5337717871103154852)
XLA Ops:
  0.0 53.0 %shard_map.118 = bf16[64,32,128]{2,1,0:T(8,128)(2,1)} custom-call(bf16[64,32,128]{2,1,0:T(8,128)(2,1)} %refs_0_.1, s32[64,64]{1,0:T(8,128)} %refs_1_.1, f32[1,128]{1,0:T(1,128)} %bitcast.4, f32[1,128]{1,0:T(1,128)} %bitcast.5, bf16[128,128]{1,0:T(8,128)(2,1)} %refs_4_.1, bf16[128,128]{1,0:T(8,128)(2,1)} %refs_5_.1, bf16[128,128]{1,0:T(8,128)(2,1)} %refs_6_.1, ...), custom_call_target="tpu_custom_call" | custom-call | tf_op jit(solution)/shard_map/pallas_call | solution.py:408
  53.0 1.9 %copy.14 = bf16[64,32,128]{2,1,0:T(8,128)(2,1)} copy(bf16[64,32,128]{2,1,0:T(8,128)(2,1)} %shard_map.118) | data formatting | bytes 1048576

commit v3 on v2

--- a/solution.py
+++ b/solution.py
@@ -33,10 +33,10 @@
 
 def body(
     nr, nc, parts, operands, held, updated,
-    fetched, normed, stage, gates, mask, left_w, right_w, means, scales,
+    fetched, normed, stage, gates, mask, left_w, right_w, means, scales, gain, shift, out_w,
     left_send, right_send, left_all, right_all, cross_send, cross_all,
     left_far, far_send,
-    ls, lr, rs, rr, xs, xr, zs, zr, fs, fr, gs, gr,
+    ls, lr, rs, rr, xs, xr, zs, zr, fs, fr, gs,
 ):
     fetches = [
         pltpu.make_async_copy(source, target, fetched.at[n])
@@ -55,6 +55,10 @@
     r = lax.axis_index("row")
     c = lax.axis_index("chan")
 
+    first, last = r == 0, r == nr - 1
+    inner = jnp.logical_not(first | last)
+    share, split = nr // 2, nc // 2
+
     barrier = pltpu.get_barrier_semaphore()
 
     @pl.loop(1, nc)
@@ -71,12 +75,28 @@
     def _():
         pl.semaphore_signal(barrier, inc=1, device_id={"row": r + 1}, device_id_type=MESH)
 
+    def greet(row):
+        @pl.loop(1, nc)
+        def _(d):
+            pl.semaphore_signal(
+                barrier, inc=1, device_id={"row": row, "chan": lax.rem(c + d, nc)},
+                device_id_type=MESH,
+            )
+
+    @pl.when(last & (c < split))
+    def _():
+        greet(r - 1)
+
+    @pl.when(first & (c >= split))
+    def _():
+        greet(r + 1)
+
     for n in (0, 2, 3):
         fetches[n].wait()
 
     group = 8
 
-    @pl.loop(0, rows // group)
+    @pl.loop(0, rows // group, unroll=2)
     def _(g):
         v = pair[pl.ds(g * group, group)].astype(F32).reshape(group * cols, width)
         m = jnp.mean(v, axis=1, keepdims=True)
@@ -177,22 +197,16 @@
 
     edges(right_w, right_send)
     pl.semaphore_wait(
-        barrier, nc - 1 + jnp.where(r > 0, 1, 0) + jnp.where(r < nr - 1, 1, 0)
+        barrier,
+        nc - 1 + jnp.where(r > 0, 1, 0) + jnp.where(r < nr - 1, 1, 0)
+        + jnp.where(r == nr - 2, split - jnp.where(c < split, 1, 0), 0)
+        + jnp.where(r == 1, nc - split - jnp.where(c >= split, 1, 0), 0),
     )
     for q in range(parts):
         each_peer(lambda d: right_copy(d, q).start())
     right_all[r, :, own_cols, :] = right_send[pl.ds(c * mine, mine)]
 
-    edges(left_w, left_send)
-    for q in range(parts):
-        each_peer(lambda d: left_copy(d, q).start())
-    left_all[:, own_cols, :] = left_send[pl.ds(c * mine, mine)]
-
     lane = lax.broadcasted_iota(jnp.int32, (rows, width), 1)
-
-    first, last = r == 0, r == nr - 1
-    share = nr // 2
-    low_part, high_part = pl.ds(0, share * rows), pl.ds(share * rows, (nr - share) * rows)
 
     def left_over(q, way):
         return pltpu.make_async_remote_copy(
@@ -201,26 +215,42 @@
             device_id={"row": r + 1 - 2 * way}, device_id_type=MESH,
         )
 
-    def products_over(q, way):
-        there = high_part if way else low_part
-        return pltpu.make_async_remote_copy(
-            src_ref=far_send.at[part_of(q), there], dst_ref=cross_send.at[part_of(q), there],
-            send_sem=gs.at[q], recv_sem=gr.at[q],
-            device_id={"row": r + 1 - 2 * way}, device_id_type=MESH,
-        )
+    def far_copy(d, q, way):
+        to = lax.rem(c + d, nc)
+        return pltpu.make_async_remote_copy(
+            src_ref=far_send.at[part_of(q), pl.ds(pl.multiple_of(to * cols, cols), cols), :],
+            dst_ref=cross_all.at[pl.ds(c * mine + q * each, each)],
+            send_sem=gs.at[d, q], recv_sem=xr.at[d, q],
+            device_id={"row": r + 1 - 2 * way, "chan": to}, device_id_type=MESH,
+        )
+
+    def each_far(way, act):
+        @pl.loop(0, nc)
+        def _(d):
+            to = lax.rem(c + d, nc)
+
+            @pl.when((to >= split) if way else (to < split))
+            def _():
+                act(d)
+
+    def is_near(to):
+        return inner | (last & (to >= split)) | (first & (to < split))
+
+    def each_near(act):
+        @pl.loop(1, nc)
+        def _(d):
+            @pl.when(is_near(lax.rem(c + d, nc)))
+            def _():
+                act(d)
 
     def multiply(q, start, stop, left, into):
-        @pl.loop(start, stop)
+        @pl.loop(start, stop, unroll=2)
         def _(b):
             for h in range(q * each, (q + 1) * each):
                 both = contract(right_all[b, h], left[h], 0, 0)
                 x = jnp.where(lane < half, both[:half], both[half:]).astype(BF16)
                 into[h, pl.ds(pl.multiple_of(b * rows, rows), rows), :] = x
 
-    def send_products(q):
-        each_peer(lambda d: cross_copy(d, q).start())
-        cross_all[pl.ds(c * mine + q * each, each)] = cross_send[part_of(q), own_cols, :]
-
     def own_products(q):
         @pl.when(first)
         def _():
@@ -230,34 +260,29 @@
         def _():
             multiply(q, share, nr, left_all, cross_send)
 
-        @pl.when(jnp.logical_not(first | last))
+        @pl.when(inner)
         def _():
             each_peer(lambda d: left_copy(d, q).wait_recv())
             multiply(q, 0, nr, left_all, cross_send)
-            send_products(q)
+
+        each_near(lambda d: cross_copy(d, q).start())
+
+        @pl.when(is_near(c))
+        def _():
+            cross_all[pl.ds(c * mine + q * each, each)] = cross_send[part_of(q), own_cols, :]
 
     def far_products(q):
         @pl.when(r == 1)
         def _():
             left_over(q, 0).wait_recv()
             multiply(q, share, nr, left_far, far_send)
-            products_over(q, 1).start()
+            each_far(1, lambda d: far_copy(d, q, 1).start())
 
         @pl.when(r == nr - 2)
         def _():
             left_over(q, 1).wait_recv()
             multiply(q, 0, share, left_far, far_send)
-            products_over(q, 0).start()
-
-        @pl.when(first)
-        def _():
-            products_over(q, 1).wait_recv()
-            send_products(q)
-
-        @pl.when(last)
-        def _():
-            products_over(q, 0).wait_recv()
-            send_products(q)
+            each_far(0, lambda d: far_copy(d, q, 0).start())
 
     def pass_on(block, q, way, arrives):
         if way == 0:
@@ -276,19 +301,31 @@
             def _():
                 row_copy(block, q, way).start()
 
+    def own_on(q):
+        each_peer(lambda d: right_copy(d, q).wait_recv())
+        pass_on(r, q, 0, False)
+        pass_on(r, q, 1, False)
+
+    @pl.loop(0, cols, unroll=4)
+    def _(k):
+        gates[k] = jax.nn.sigmoid(contract(at_column(k), out_gate[...], 1, 0))
+
+    own_on(0)
+
+    edges(left_w, left_send)
+    for q in range(parts):
+        each_peer(lambda d: left_copy(d, q).start())
+    left_all[:, own_cols, :] = left_send[pl.ds(c * mine, mine)]
+
+    lane_h = lax.broadcasted_iota(jnp.int32, (half, width), 1)
+    g = column(out_gain)
+    s = column(out_shift)
+    gain[...] = jnp.where(lane_h < half, g[:half], g[half:])
+    shift[...] = jnp.where(lane_h < half, s[:half], s[half:])
+    out_w[...] = jnp.concatenate([out_proj[:half], out_proj[half:]], axis=1)
+
     @pl.when(first | last)
     def _():
-        def right_on(q):
-            each_peer(lambda d: right_copy(d, q).wait_recv())
-
-            @pl.when(first)
-            def _():
-                row_copy(r, q, 0).start()
-
-            @pl.when(last)
-            def _():
-                row_copy(r, q, 1).start()
-
         def left_on(q):
             each_peer(lambda d: left_copy(d, q).wait_recv())
 
@@ -300,62 +337,60 @@
             def _():
                 left_over(q, 1).start()
 
-        for q in range(parts + 1):
-            if q < parts:
-                right_on(q)
-            if q > 0:
-                left_on(q - 1)
+        for q in range(1, parts):
+            own_on(q)
+            left_on(q - 1)
+        left_on(parts - 1)
 
     for t in range(parts + nr - 1):
-        if t < parts:
-            @pl.when(jnp.logical_not(first | last))
-            def _():
-                each_peer(lambda d: right_copy(d, t).wait_recv())
-                pass_on(r, t, 0, False)
-                pass_on(r, t, 1, False)
+        if 0 < t < parts:
+            @pl.when(inner)
+            def _():
+                own_on(t)
         for s in range(1, nr - 1):
             q = t - s
             if 0 <= q < parts:
                 pass_on(r - s, q, 0, True)
                 pass_on(r + s, q, 1, True)
-        if t == 0:
-            @pl.loop(0, cols, unroll=4)
-            def _(k):
-                gates[k] = jax.nn.sigmoid(contract(at_column(k), out_gate[...], 1, 0))
-
         if 0 <= t - (nr - 2) < parts:
             own_products(t - (nr - 2))
         if t >= nr - 1:
             far_products(t - (nr - 1))
 
+    total = jnp.zeros((cols, width), F32)
+    squares = total
     for q in range(parts):
         each_peer(lambda d: cross_copy(d, q).wait_recv())
 
-    def add_up(h, sums):
-        x = cross_all[h].astype(F32)
-        stage[pl.ds(pl.multiple_of(h * cols, cols), cols), :] = x
-        return sums[0] + x, sums[1] + x * x
-
-    zero = jnp.zeros((cols, width), F32)
-    total, squares = lax.fori_loop(0, half, add_up, (zero, zero), unroll=4)
+        @pl.when(first & (c >= split))
+        def _():
+            far_copy(0, q, 0).wait_recv()
+
+        @pl.when(last & (c < split))
+        def _():
+            far_copy(0, q, 1).wait_recv()
+
+        def add_up(p, sums):
+            for e in range(each):
+                h = p * mine + q * each + e
+                x = cross_all[h].astype(F32)
+                stage[pl.ds(pl.multiple_of(h * cols, cols), cols), :] = x
+                sums = sums[0] + x, sums[1] + x * x
+            return sums
+
+        total, squares = lax.fori_loop(0, nc, add_up, (total, squares), unroll=4)
+
     total = total + pltpu.roll(total, half, 1)
     squares = squares + pltpu.roll(squares, half, 1)
     m = total / width
     means[...] = m
     scales[...] = lax.rsqrt(squares / width - m * m + epsilon)
 
-    lane_h = lax.broadcasted_iota(jnp.int32, (half, width), 1)
-    g = column(out_gain)
-    s = column(out_shift)
-    gain = jnp.where(lane_h < half, g[:half], g[half:])
-    shift = jnp.where(lane_h < half, s[:half], s[half:])
-    w_out = jnp.concatenate([out_proj[:half], out_proj[half:]], axis=1)
-
     @pl.loop(0, cols, unroll=4)
     def _(j):
         x = stage[pl.ds(j, half, stride=cols), :]
-        x = (x - means[pl.ds(j, 1), :]) * scales[pl.ds(j, 1), :] * gain + shift
-        y = contract(x.astype(BF16), w_out, 0, 0)
+        x = (x - means[pl.ds(j, 1), :]) * scales[pl.ds(j, 1), :] * gain[...] + shift[...]
+        y = contract(x.astype(BF16), out_w[...], 0, 0)
         normed[pl.ds(j, rows, stride=cols), :] = gates[j] * (y[:half, :width] + y[half:, width:])
 
     @pl.loop(0, rows // group)
@@ -367,18 +402,22 @@
         def sent(d):
             right_copy(d, q).wait_send()
             left_copy(d, q).wait_send()
-            cross_copy(d, q).wait_send()
 
         each_peer(sent)
+        each_near(lambda d: cross_copy(d, q).wait_send())
+
+        @pl.when(r == 1)
+        def _():
+            each_far(1, lambda d: far_copy(d, q, 1).wait_send())
+
+        @pl.when(r == nr - 2)
+        def _():
+            each_far(0, lambda d: far_copy(d, q, 0).wait_send())
 
     for q in range(parts):
         @pl.when(first | last)
         def _():
             left_over(q, 0).wait_send()
-
-        @pl.when((r == 1) | (r == nr - 2))
-        def _():
-            products_over(q, 0).wait_send()
 
         @pl.loop(0, nr)
         def _(block):
@@ -395,7 +434,7 @@
           out_gain, out_shift, out_gate, out_proj):
     rows, cols, width = pair.shape
     half = width // 2
-    assert rows == half and nr >= 4 and nr % 2 == 0
+    assert rows == half and nr >= 4 and nr % 2 == 0 and nc % 2 == 0
     mine = half // nc
     parts = math.gcd(mine, 4)
     total = cols * nc
@@ -408,7 +447,7 @@
     return pl.pallas_call(
         functools.partial(kernel, nr, nc, parts),
         out_shape=jax.ShapeDtypeStruct(pair.shape, BF16),
-        in_specs=[pl.BlockSpec(memory_space=pl.ANY)] * 12,
+        in_specs=[pl.BlockSpec(memory_space=pltpu.HBM)] * 12,
         out_specs=pl.BlockSpec(memory_space=pltpu.VMEM),
         scratch_shapes=[vmem(a.shape, a.dtype) for a in operands] + [
             dma((len(operands),)),
@@ -420,6 +459,9 @@
             vmem((width, 2 * width), BF16),
             vmem((cols, width), F32),
             vmem((cols, width), F32),
+            vmem((half, width), F32),
+            vmem((half, width), F32),
+            vmem((half, 2 * width), BF16),
             vmem((half, cols, width), BF16),
             vmem((half, cols, width), BF16),
             vmem((mine, total, width), BF16),
@@ -432,12 +474,12 @@
             dma((nc, parts)), dma((nc, parts)),
             dma((nc, parts)), dma((nc, parts)),
             dma((2, nr, parts)), dma((nr, parts)),
-            dma((parts,)), dma((parts,)), dma((parts,)), dma((parts,)),
+            dma((parts,)), dma((parts,)), dma((nc, parts)),
         ],
         compiler_params=pltpu.CompilerParams(
-            collective_id=0, has_side_effects=True, vmem_limit_bytes=60 * 1024 * 1024
+            collective_id=0, has_side_effects=True, vmem_limit_bytes=48 * 1024 * 1024
         ),
-    )(*operands)
+    )(*[pltpu.with_memory_space_constraint(a, pltpu.HBM) for a in operands])
 
 
 def solution(mesh):

time: 55 us -> 48.4 us (0.88)
  the two profiles are of different devices: /device:TPU:0 before, /device:TPU:5 now
where the time goes in v3:
time: 48.4 us; the launch traced here: 48.2 us
  Pallas kernels  47.4 us (98%)
  local copies, waits for them, and re-layouts  0.8 us (2%)
    pallas_call x1, Pallas kernels, local(): pl.pallas_call(functools.partial(kernel, nr, nc, parts), out_shape=jax.Sh...  47.4 us

profile of v3, /device:TPU:5, one launch (start us, length us, event | category | flops | bytes accessed | tf_op | source)
XLA Modules:
  0.0 48.2 jit_solution(4869931394662928280)
XLA Ops:
  0.0 47.4 %shard_map.118 = bf16[64,32,128]{2,1,0:T(8,128)(2,1)S(1)} custom-call(bf16[64,32,128]{2,1,0:T(8,128)(2,1)} %refs_0_.1, s32[64,64]{1,0:T(8,128)} %refs_1_.1, f32[1,128]{1,0:T(1,128)} %bitcast.4, f32[1,128]{1,0:T(1,128)} %bitcast.5, bf16[128,128]{1,0:T(8,128)(2,1)} %refs_4_.1, bf16[128,128]{1,0:T(8,128)(2,1)} %refs_5_.1, bf16[128,128]{1,0:T(8,128)(2,1)} %refs_6_.1, ...), custom_call_target="tpu_custom_call" | custom-call | tf_op jit(solution)/shard_map/pallas_call | solution.py:447
  47.4 0.8 %copy.14 = bf16[64,32,128]{2,1,0:T(8,128)(2,1)} copy(bf16[64,32,128]{2,1,0:T(8,128)(2,1)S(1)} %shard_map.118) | data formatting | bytes 1048576

commit v4 on v3

--- a/solution.py
+++ b/solution.py
@@ -135,7 +135,7 @@
         w = w_ref[...]
         empty = jnp.zeros((rows, width), BF16)
 
-        @pl.loop(0, cols, unroll=4)
+        @pl.loop(0, cols, unroll=8)
         def _(k):
             n = at_column(k)
             both = jnp.concatenate(
@@ -158,7 +158,7 @@
         return pltpu.make_async_remote_copy(
             src_ref=right_send.at[pl.ds(to * mine + q * each, each)],
             dst_ref=right_all.at[r, part_of(q), pl.ds(pl.multiple_of(c * cols, cols), cols), :],
-            send_sem=rs.at[d, q], recv_sem=rr.at[d, q],
+            send_sem=rs, recv_sem=rr.at[q],
             device_id={"chan": to}, device_id_type=MESH,
         )
 
@@ -167,7 +167,7 @@
         return pltpu.make_async_remote_copy(
             src_ref=left_send.at[pl.ds(to * mine + q * each, each)],
             dst_ref=left_all.at[part_of(q), pl.ds(pl.multiple_of(c * cols, cols), cols), :],
-            send_sem=ls.at[d, q], recv_sem=lr.at[d, q],
+            send_sem=ls, recv_sem=lr.at[q],
             device_id={"chan": to}, device_id_type=MESH,
         )
 
@@ -176,7 +176,7 @@
         return pltpu.make_async_remote_copy(
             src_ref=cross_send.at[part_of(q), pl.ds(pl.multiple_of(to * cols, cols), cols), :],
             dst_ref=cross_all.at[pl.ds(c * mine + q * each, each)],
-            send_sem=xs.at[d, q], recv_sem=xr.at[d, q],
+            send_sem=xs, recv_sem=xr.at[q],
             device_id={"chan": to}, device_id_type=MESH,
         )
 
@@ -184,9 +184,23 @@
         return pltpu.make_async_remote_copy(
             src_ref=right_all.at[block, part_of(q)],
             dst_ref=right_all.at[block, part_of(q)],
-            send_sem=zs.at[way, block, q], recv_sem=zr.at[block, q],
+            send_sem=zs.at[way, block], recv_sem=zr.at[block, q],
             device_id={"row": r + 1 - 2 * way}, device_id_type=MESH,
         )
+
+    def all_bytes(ref, send_sem, recv_sem):
+        return pltpu.make_async_remote_copy(
+            src_ref=ref, dst_ref=ref, send_sem=send_sem, recv_sem=recv_sem,
+            device_id={"chan": lax.rem(c + 1, nc)}, device_id_type=MESH,
+        )
+
+    others = pl.ds(0, (nc - 1) * cols)
+
+    def right_wait(q):
+        all_bytes(right_all.at[r, part_of(q), others, :], rs, rr.at[q]).wait_recv()
+
+    def left_wait(q):
+        all_bytes(left_all.at[part_of(q), others, :], ls, lr.at[q]).wait_recv()
 
     def each_peer(act):
         @pl.loop(1, nc)
@@ -211,7 +225,7 @@
     def left_over(q, way):
         return pltpu.make_async_remote_copy(
             src_ref=left_all.at[part_of(q)], dst_ref=left_far.at[part_of(q)],
-            send_sem=fs.at[q], recv_sem=fr.at[q],
+            send_sem=fs, recv_sem=fr.at[q],
             device_id={"row": r + 1 - 2 * way}, device_id_type=MESH,
         )
 
@@ -220,7 +234,7 @@
         return pltpu.make_async_remote_copy(
             src_ref=far_send.at[part_of(q), pl.ds(pl.multiple_of(to * cols, cols), cols), :],
             dst_ref=cross_all.at[pl.ds(c * mine + q * each, each)],
-            send_sem=gs.at[d, q], recv_sem=xr.at[d, q],
+            send_sem=gs, recv_sem=xr.at[q],
             device_id={"row": r + 1 - 2 * way, "chan": to}, device_id_type=MESH,
         )
 
@@ -262,7 +276,7 @@
 
         @pl.when(inner)
         def _():
-            each_peer(lambda d: left_copy(d, q).wait_recv())
+            left_wait(q)
             multiply(q, 0, nr, left_all, cross_send)
 
         each_near(lambda d: cross_copy(d, q).start())
@@ -302,11 +316,11 @@
                 row_copy(block, q, way).start()
 
     def own_on(q):
-        each_peer(lambda d: right_copy(d, q).wait_recv())
+        right_wait(q)
         pass_on(r, q, 0, False)
         pass_on(r, q, 1, False)
 
-    @pl.loop(0, cols, unroll=4)
+    @pl.loop(0, cols, unroll=8)
     def _(k):
         gates[k] = jax.nn.sigmoid(contract(at_column(k), out_gate[...], 1, 0))
 
@@ -327,7 +341,7 @@
     @pl.when(first | last)
     def _():
         def left_on(q):
-            each_peer(lambda d: left_copy(d, q).wait_recv())
+            left_wait(q)
 
             @pl.when(first)
             def _():
@@ -360,15 +374,13 @@
     total = jnp.zeros((cols, width), F32)
     squares = total
     for q in range(parts):
-        each_peer(lambda d: cross_copy(d, q).wait_recv())
-
-        @pl.when(first & (c >= split))
-        def _():
-            far_copy(0, q, 0).wait_recv()
-
-        @pl.when(last & (c < split))
-        def _():
-            far_copy(0, q, 1).wait_recv()
+        @pl.when(is_near(c))
+        def _():
+            all_bytes(cross_all.at[pl.ds(0, (nc - 1) * each)], xs, xr.at[q]).wait_recv()
+
+        @pl.when(jnp.logical_not(is_near(c)))
+        def _():
+            all_bytes(cross_all.at[pl.ds(0, nc * each)], xs, xr.at[q]).wait_recv()
 
         def add_up(p, sums):
             for e in range(each):
@@ -386,7 +398,7 @@
     means[...] = m
     scales[...] = lax.rsqrt(squares / width - m * m + epsilon)
 
-    @pl.loop(0, cols, unroll=4)
+    @pl.loop(0, cols, unroll=8)
     def _(j):
         x = stage[pl.ds(j, half, stride=cols), :]
         x = (x - means[pl.ds(j, 1), :]) * scales[pl.ds(j, 1), :] * gain[...] + shift[...]
@@ -398,43 +410,49 @@
         at = pl.ds(pl.multiple_of(g * group * cols, group * cols), group * cols)
         updated[pl.ds(g * group, group)] = normed[at, :].astype(BF16).reshape(group, cols, width)
 
-    for q in range(parts):
-        def sent(d):
-            right_copy(d, q).wait_send()
-            left_copy(d, q).wait_send()
-
-        each_peer(sent)
-        each_near(lambda d: cross_copy(d, q).wait_send())
-
-        @pl.when(r == 1)
-        def _():
-            each_far(1, lambda d: far_copy(d, q, 1).wait_send())
-
-        @pl.when(r == nr - 2)
-        def _():
-            each_far(0, lambda d: far_copy(d, q, 0).wait_send())
-
-    for q in range(parts):
-        @pl.when(first | last)
-        def _():
-            left_over(q, 0).wait_send()
-
-        @pl.loop(0, nr)
-        def _(block):
-            @pl.when((block <= r) & ((r < nr - 2) | ((r == nr - 2) & (block >= share))))
-            def _():
-                row_copy(block, q, 0).wait_send()
-
-            @pl.when((block >= r) & ((r > 1) | ((r == 1) & (block < share))))
-            def _():
-                row_copy(block, q, 1).wait_send()
+    all_bytes(right_send.at[pl.ds(0, (nc - 1) * mine)], rs, rr.at[0]).wait_send()
+    all_bytes(left_send.at[pl.ds(0, (nc - 1) * mine)], ls, lr.at[0]).wait_send()
+
+    def products_sent(count):
+        there = pl.ds(0, count * cols)
+        all_bytes(cross_send.at[:, there, :], xs, xr.at[0]).wait_send()
+
+    @pl.when(inner)
+    def _():
+        products_sent(nc - 1)
+
+    @pl.when((first | last) & is_near(c))
+    def _():
+        products_sent(split - 1)
+
+    @pl.when(jnp.logical_not(is_near(c)))
+    def _():
+        products_sent(split)
+
+    @pl.when((r == 1) | (r == nr - 2))
+    def _():
+        all_bytes(far_send.at[:, pl.ds(0, split * cols), :], gs, xr.at[0]).wait_send()
+
+    @pl.when(first | last)
+    def _():
+        all_bytes(left_all, fs, fr.at[0]).wait_send()
+
+    @pl.loop(0, nr)
+    def _(block):
+        @pl.when((block <= r) & ((r < nr - 2) | ((r == nr - 2) & (block >= share))))
+        def _():
+            all_bytes(right_all.at[block], zs.at[0, block], zr.at[block, 0]).wait_send()
+
+        @pl.when((block >= r) & ((r > 1) | ((r == 1) & (block < share))))
+        def _():
+            all_bytes(right_all.at[block], zs.at[1, block], zr.at[block, 0]).wait_send()
 
 
 def local(nr, nc, pair, tile_mask, in_gain, in_shift, left_gate, left_proj, right_gate, right_proj,
           out_gain, out_shift, out_gate, out_proj):
     rows, cols, width = pair.shape
     half = width // 2
-    assert rows == half and nr >= 4 and nr % 2 == 0 and nc % 2 == 0
+    assert rows == half and nr >= 4 and nr % 2 == 0 and nc % 2 == 0 and nc >= 4
     mine = half // nc
     parts = math.gcd(mine, 4)
     total = cols * nc
@@ -470,11 +488,11 @@
             vmem((half, cols, width), BF16),
             vmem((mine, total, width), BF16),
             vmem((mine, rows * nr, width), BF16),
-            dma((nc, parts)), dma((nc, parts)),
-            dma((nc, parts)), dma((nc, parts)),
-            dma((nc, parts)), dma((nc, parts)),
-            dma((2, nr, parts)), dma((nr, parts)),
-            dma((parts,)), dma((parts,)), dma((nc, parts)),
+            dma, dma((parts,)),
+            dma, dma((parts,)),
+            dma, dma((parts,)),
+            dma((2, nr)), dma((nr, parts)),
+            dma, dma((parts,)), dma,
         ],
         compiler_params=pltpu.CompilerParams(
             collective_id=0, has_side_effects=True, vmem_limit_bytes=48 * 1024 * 1024

time: 48.4 us -> 43.5 us (0.90)
  Pallas kernels: 47.4 us -> 42.6 us
    pallas_call x1, Pallas kernels: 47.4 us -> 42.6 us  [local(): pl.pallas_call(functools.partial(kernel, nr, nc, parts), out_shape=jax.Sh...]
where the time goes in v4:
time: 43.5 us; the launch traced here: 43.4 us
  Pallas kernels  42.6 us (98%)
  local copies, waits for them, and re-layouts  0.8 us (2%)
    pallas_call x1, Pallas kernels, local(): pl.pallas_call(functools.partial(kernel, nr, nc, parts), out_shape=jax.Sh...  42.6 us

profile of v4, /device:TPU:5, one launch (start us, length us, event | category | flops | bytes accessed | tf_op | source)
XLA Modules:
  0.0 43.4 jit_solution(4494958617037681531)
XLA Ops:
  0.0 42.6 %shard_map.118 = bf16[64,32,128]{2,1,0:T(8,128)(2,1)S(1)} custom-call(bf16[64,32,128]{2,1,0:T(8,128)(2,1)} %refs_0_.1, s32[64,64]{1,0:T(8,128)} %refs_1_.1, f32[1,128]{1,0:T(1,128)} %bitcast.4, f32[1,128]{1,0:T(1,128)} %bitcast.5, bf16[128,128]{1,0:T(8,128)(2,1)} %refs_4_.1, bf16[128,128]{1,0:T(8,128)(2,1)} %refs_5_.1, bf16[128,128]{1,0:T(8,128)(2,1)} %refs_6_.1, ...), custom_call_target="tpu_custom_call" | custom-call | tf_op jit(solution)/shard_map/pallas_call | solution.py:465
  42.6 0.8 %copy.14 = bf16[64,32,128]{2,1,0:T(8,128)(2,1)} copy(bf16[64,32,128]{2,1,0:T(8,128)(2,1)S(1)} %shard_map.118) | data formatting | bytes 1048576

commit v5 on v4

--- a/solution.py
+++ b/solution.py
@@ -1,5 +1,4 @@
 import functools
-import math
 
 import jax
 import jax.numpy as jnp
@@ -24,15 +23,15 @@
 
 
 def kernel(
-    nr, nc, parts,
+    nr, nc, sizes,
     *refs,
 ):
     operands, (updated,), held, rest = refs[:12], refs[12:13], refs[13:25], refs[25:]
-    body(nr, nc, parts, operands, held, updated, *rest)
+    body(nr, nc, sizes, operands, held, updated, *rest)
 
 
 def body(
-    nr, nc, parts, operands, held, updated,
+    nr, nc, sizes, operands, held, updated,
     fetched, normed, stage, gates, mask, left_w, right_w, means, scales, gain, shift, out_w,
     left_send, right_send, left_all, right_all, cross_send, cross_all,
     left_far, far_send,
@@ -49,7 +48,10 @@
     rows, cols, width = pair.shape
     half = width // 2
     mine = half // nc
-    each = mine // parts
+    begins = [sum(sizes[:q]) for q in range(len(sizes))]
+    parts = len(sizes)
+    middle = parts // 2
+    groups = [(0, begins[middle]), (begins[middle], mine - begins[middle])]
     tiles = tile_mask.shape[0]
     tile = rows * nr // tiles
     r = lax.axis_index("row")
@@ -125,8 +127,6 @@
 
     right_w[:half] = paired(right_gate)
     right_w[half:] = paired(right_proj)
-    left_w[:half] = paired(left_gate)
-    left_w[half:] = paired(left_proj)
 
     def at_column(k):
         return normed[pl.ds(k, rows, stride=cols), :].astype(BF16)
@@ -151,23 +151,24 @@
             send[pl.ds(g * group, group)] = stage[at, :].astype(BF16).reshape(group, cols, width)
 
     def part_of(q):
-        return pl.ds(q * each, each)
+        return pl.ds(begins[q], sizes[q])
 
     def right_copy(d, q):
         to = lax.rem(c + d, nc)
         return pltpu.make_async_remote_copy(
-            src_ref=right_send.at[pl.ds(to * mine + q * each, each)],
+            src_ref=right_send.at[pl.ds(to * mine + begins[q], sizes[q])],
             dst_ref=right_all.at[r, part_of(q), pl.ds(pl.multiple_of(c * cols, cols), cols), :],
             send_sem=rs, recv_sem=rr.at[q],
             device_id={"chan": to}, device_id_type=MESH,
         )
 
-    def left_copy(d, q):
+    def left_copy(d, n):
         to = lax.rem(c + d, nc)
-        return pltpu.make_async_remote_copy(
-            src_ref=left_send.at[pl.ds(to * mine + q * each, each)],
-            dst_ref=left_all.at[part_of(q), pl.ds(pl.multiple_of(c * cols, cols), cols), :],
-            send_sem=ls, recv_sem=lr.at[q],
+        begin, size = groups[n]
+        return pltpu.make_async_remote_copy(
+            src_ref=left_send.at[pl.ds(to * mine + begin, size)],
+            dst_ref=left_all.at[pl.ds(begin, size), pl.ds(pl.multiple_of(c * cols, cols), cols), :],
+            send_sem=ls, recv_sem=lr.at[n],
             device_id={"chan": to}, device_id_type=MESH,
         )
 
@@ -175,7 +176,7 @@
         to = lax.rem(c + d, nc)
         return pltpu.make_async_remote_copy(
             src_ref=cross_send.at[part_of(q), pl.ds(pl.multiple_of(to * cols, cols), cols), :],
-            dst_ref=cross_all.at[pl.ds(c * mine + q * each, each)],
+            dst_ref=cross_all.at[pl.ds(c * mine + begins[q], sizes[q])],
             send_sem=xs, recv_sem=xr.at[q],
             device_id={"chan": to}, device_id_type=MESH,
         )
@@ -200,7 +201,9 @@
         all_bytes(right_all.at[r, part_of(q), others, :], rs, rr.at[q]).wait_recv()
 
     def left_wait(q):
-        all_bytes(left_all.at[part_of(q), others, :], ls, lr.at[q]).wait_recv()
+        for n, (begin, size) in enumerate(groups):
+            if begins[q] == begin:
+                all_bytes(left_all.at[pl.ds(begin, size), others, :], ls, lr.at[n]).wait_recv()
 
     def each_peer(act):
         @pl.loop(1, nc)
@@ -218,6 +221,8 @@
     )
     for q in range(parts):
         each_peer(lambda d: right_copy(d, q).start())
+    left_w[:half] = paired(left_gate)
+    left_w[half:] = paired(left_proj)
     right_all[r, :, own_cols, :] = right_send[pl.ds(c * mine, mine)]
 
     lane = lax.broadcasted_iota(jnp.int32, (rows, width), 1)
@@ -233,7 +238,7 @@
         to = lax.rem(c + d, nc)
         return pltpu.make_async_remote_copy(
             src_ref=far_send.at[part_of(q), pl.ds(pl.multiple_of(to * cols, cols), cols), :],
-            dst_ref=cross_all.at[pl.ds(c * mine + q * each, each)],
+            dst_ref=cross_all.at[pl.ds(c * mine + begins[q], sizes[q])],
             send_sem=gs, recv_sem=xr.at[q],
             device_id={"row": r + 1 - 2 * way, "chan": to}, device_id_type=MESH,
         )
@@ -258,14 +263,14 @@
                 act(d)
 
     def multiply(q, start, stop, left, into):
-        @pl.loop(start, stop, unroll=2)
+        @pl.loop(start, stop)
         def _(b):
-            for h in range(q * each, (q + 1) * each):
+            for h in range(begins[q], begins[q] + sizes[q]):
                 both = contract(right_all[b, h], left[h], 0, 0)
                 x = jnp.where(lane < half, both[:half], both[half:]).astype(BF16)
                 into[h, pl.ds(pl.multiple_of(b * rows, rows), rows), :] = x
 
-    def own_products(q):
+    def early_products(q):
         @pl.when(first)
         def _():
             multiply(q, 0, share, left_all, cross_send)
@@ -277,13 +282,31 @@
         @pl.when(inner)
         def _():
             left_wait(q)
-            multiply(q, 0, nr, left_all, cross_send)
-
+            multiply(q, jnp.where(r == nr - 2, 1, 0), nr - jnp.where(r == 1, 1, 0), left_all, cross_send)
+
+        @pl.when(first | last)
+        def _():
+            send_products(q)
+
+    def late_products(q):
+        @pl.when(r == 1)
+        def _():
+            multiply(q, nr - 1, nr, left_all, cross_send)
+
+        @pl.when(r == nr - 2)
+        def _():
+            multiply(q, 0, 1, left_all, cross_send)
+
+        @pl.when(inner)
+        def _():
+            send_products(q)
+
+    def send_products(q):
         each_near(lambda d: cross_copy(d, q).start())
 
         @pl.when(is_near(c))
         def _():
-            cross_all[pl.ds(c * mine + q * each, each)] = cross_send[part_of(q), own_cols, :]
+            cross_all[pl.ds(c * mine + begins[q], sizes[q])] = cross_send[part_of(q), own_cols, :]
 
     def far_products(q):
         @pl.when(r == 1)
@@ -327,8 +350,8 @@
     own_on(0)
 
     edges(left_w, left_send)
-    for q in range(parts):
-        each_peer(lambda d: left_copy(d, q).start())
+    for n in range(len(groups)):
+        each_peer(lambda d: left_copy(d, n).start())
     left_all[:, own_cols, :] = left_send[pl.ds(c * mine, mine)]
 
     lane_h = lax.broadcasted_iota(jnp.int32, (half, width), 1)
@@ -356,7 +379,7 @@
             left_on(q - 1)
         left_on(parts - 1)
 
-    for t in range(parts + nr - 1):
+    for t in range(parts + nr - 2):
         if 0 < t < parts:
             @pl.when(inner)
             def _():
@@ -366,25 +389,26 @@
             if 0 <= q < parts:
                 pass_on(r - s, q, 0, True)
                 pass_on(r + s, q, 1, True)
-        if 0 <= t - (nr - 2) < parts:
-            own_products(t - (nr - 2))
-        if t >= nr - 1:
-            far_products(t - (nr - 1))
+        if t >= nr - 2:
+            far_products(t - (nr - 2))
+            late_products(t - (nr - 2))
+        if 0 <= t - (nr - 3) < parts:
+            early_products(t - (nr - 3))
 
     total = jnp.zeros((cols, width), F32)
     squares = total
     for q in range(parts):
         @pl.when(is_near(c))
         def _():
-            all_bytes(cross_all.at[pl.ds(0, (nc - 1) * each)], xs, xr.at[q]).wait_recv()
+            all_bytes(cross_all.at[pl.ds(0, (nc - 1) * sizes[q])], xs, xr.at[q]).wait_recv()
 
         @pl.when(jnp.logical_not(is_near(c)))
         def _():
-            all_bytes(cross_all.at[pl.ds(0, nc * each)], xs, xr.at[q]).wait_recv()
+            all_bytes(cross_all.at[pl.ds(0, nc * sizes[q])], xs, xr.at[q]).wait_recv()
 
         def add_up(p, sums):
-            for e in range(each):
-                h = p * mine + q * each + e
+            for e in range(sizes[q]):
+                h = p * mine + begins[q] + e
                 x = cross_all[h].astype(F32)
                 stage[pl.ds(pl.multiple_of(h * cols, cols), cols), :] = x
                 sums = sums[0] + x, sums[1] + x * x
@@ -452,9 +476,10 @@
           out_gain, out_shift, out_gate, out_proj):
     rows, cols, width = pair.shape
     half = width // 2
-    assert rows == half and nr >= 4 and nr % 2 == 0 and nc % 2 == 0 and nc >= 4
     mine = half // nc
-    parts = math.gcd(mine, 4)
+    assert rows == half and nr >= 4 and nr % 2 == 0 and nc % 2 == 0 and nc >= 4 and mine >= 2
+    sizes = (1,) * mine if mine < 4 else (1,) + (2,) * ((mine - 2) // 2) + (1,) * (1 + mine % 2)
+    parts = len(sizes)
     total = cols * nc
     dma = pltpu.SemaphoreType.DMA
     vmem = pltpu.VMEM
@@ -463,7 +488,7 @@
         right_proj, out_gain[None], out_shift[None], out_gate, out_proj,
     )
     return pl.pallas_call(
-        functools.partial(kernel, nr, nc, parts),
+        functools.partial(kernel, nr, nc, sizes),
         out_shape=jax.ShapeDtypeStruct(pair.shape, BF16),
         in_specs=[pl.BlockSpec(memory_space=pltpu.HBM)] * 12,
         out_specs=pl.BlockSpec(memory_space=pltpu.VMEM),
@@ -488,7 +513,7 @@
             vmem((half, cols, width), BF16),
             vmem((mine, total, width), BF16),
             vmem((mine, rows * nr, width), BF16),
-            dma, dma((parts,)),
+            dma, dma((2,)),
             dma, dma((parts,)),
             dma, dma((parts,)),
             dma((2, nr)), dma((nr, parts)),

time: 43.5 us -> 44.2 us (1.016)
  no operation moved by 1% of the time
where the time goes in v5:
time: 44.2 us; the launch traced here: 43.7 us
  Pallas kernels  42.9 us (97%)
  local copies, waits for them, and re-layouts  0.8 us (2%)
    pallas_call x1, Pallas kernels, local(): pl.pallas_call(functools.partial(kernel, nr, nc, sizes), out_shape=jax.Sh...  42.9 us

profile of v5, /device:TPU:5, one launch (start us, length us, event | category | flops | bytes accessed | tf_op | source)
XLA Modules:
  0.0 43.7 jit_solution(2680163804983889449)
XLA Ops:
  0.0 42.9 %shard_map.118 = bf16[64,32,128]{2,1,0:T(8,128)(2,1)S(1)} custom-call(bf16[64,32,128]{2,1,0:T(8,128)(2,1)} %refs_0_.1, s32[64,64]{1,0:T(8,128)} %refs_1_.1, f32[1,128]{1,0:T(1,128)} %bitcast.4, f32[1,128]{1,0:T(1,128)} %bitcast.5, bf16[128,128]{1,0:T(8,128)(2,1)} %refs_4_.1, bf16[128,128]{1,0:T(8,128)(2,1)} %refs_5_.1, bf16[128,128]{1,0:T(8,128)(2,1)} %refs_6_.1, ...), custom_call_target="tpu_custom_call" | custom-call | tf_op jit(solution)/shard_map/pallas_call | solution.py:490
  42.9 0.8 %copy.14 = bf16[64,32,128]{2,1,0:T(8,128)(2,1)} copy(bf16[64,32,128]{2,1,0:T(8,128)(2,1)S(1)} %shard_map.118) | data formatting | bytes 1048576

commit v6 on v5

--- a/solution.py
+++ b/solution.py
@@ -354,6 +354,9 @@
         each_peer(lambda d: left_copy(d, n).start())
     left_all[:, own_cols, :] = left_send[pl.ds(c * mine, mine)]
 
+    for q in range(1, parts):
+        own_on(q)
+
     lane_h = lax.broadcasted_iota(jnp.int32, (half, width), 1)
     g = column(out_gain)
     s = column(out_shift)
@@ -374,26 +377,19 @@
             def _():
                 left_over(q, 1).start()
 
-        for q in range(1, parts):
-            own_on(q)
-            left_on(q - 1)
-        left_on(parts - 1)
-
-    for t in range(parts + nr - 2):
-        if 0 < t < parts:
-            @pl.when(inner)
-            def _():
-                own_on(t)
-        for s in range(1, nr - 1):
-            q = t - s
-            if 0 <= q < parts:
-                pass_on(r - s, q, 0, True)
-                pass_on(r + s, q, 1, True)
-        if t >= nr - 2:
-            far_products(t - (nr - 2))
-            late_products(t - (nr - 2))
-        if 0 <= t - (nr - 3) < parts:
-            early_products(t - (nr - 3))
+        for q in range(parts):
+            left_on(q)
+
+    for s in range(1, nr - 1):
+        for q in range(parts):
+            pass_on(r - s, q, 0, True)
+            pass_on(r + s, q, 1, True)
+            if s == nr - 2:
+                far_products(q)
+                late_products(q)
+        if s == nr - 3:
+            for q in range(parts):
+                early_products(q)
 
     total = jnp.zeros((cols, width), F32)
     squares = total

time: 44.2 us -> 42.2 us (0.955)
  Pallas kernels: 42.9 us -> 41.2 us
    pallas_call x1, Pallas kernels: 42.9 us -> 41.2 us  [local(): pl.pallas_call(functools.partial(kernel, nr, nc, sizes), out_shape=jax.Sh...]
where the time goes in v6:
time: 42.2 us; the launch traced here: 42 us
  Pallas kernels  41.2 us (98%)
  local copies, waits for them, and re-layouts  0.8 us (2%)
    pallas_call x1, Pallas kernels, local(): pl.pallas_call(functools.partial(kernel, nr, nc, sizes), out_shape=jax.Sh...  41.2 us

profile of v6, /device:TPU:5, one launch (start us, length us, event | category | flops | bytes accessed | tf_op | source)
XLA Modules:
  0.0 42.0 jit_solution(635401790892297977)
XLA Ops:
  0.0 41.2 %shard_map.118 = bf16[64,32,128]{2,1,0:T(8,128)(2,1)S(1)} custom-call(bf16[64,32,128]{2,1,0:T(8,128)(2,1)} %refs_0_.1, s32[64,64]{1,0:T(8,128)} %refs_1_.1, f32[1,128]{1,0:T(1,128)} %bitcast.4, f32[1,128]{1,0:T(1,128)} %bitcast.5, bf16[128,128]{1,0:T(8,128)(2,1)} %refs_4_.1, bf16[128,128]{1,0:T(8,128)(2,1)} %refs_5_.1, bf16[128,128]{1,0:T(8,128)(2,1)} %refs_6_.1, ...), custom_call_target="tpu_custom_call" | custom-call | tf_op jit(solution)/shard_map/pallas_call | solution.py:486
  41.2 0.8 %copy.14 = bf16[64,32,128]{2,1,0:T(8,128)(2,1)} copy(bf16[64,32,128]{2,1,0:T(8,128)(2,1)S(1)} %shard_map.118) | data formatting | bytes 1048576

commit v7 on v6

--- a/solution.py
+++ b/solution.py
@@ -32,7 +32,7 @@
 
 def body(
     nr, nc, sizes, operands, held, updated,
-    fetched, normed, stage, gates, mask, left_w, right_w, means, scales, gain, shift, out_w,
+    fetched, normed, stage, gates, mask, left_w, right_w, means, scales, gain, shift,
     left_send, right_send, left_all, right_all, cross_send, cross_all,
     left_far, far_send,
     ls, lr, rs, rr, xs, xr, zs, zr, fs, fr, gs,
@@ -121,29 +121,38 @@
     row_hot = jnp.where((ids >= low) & (ids < low + tile), 1.0, 0.0)
     mask[...] = contract(contract(col_hot, tm, 1, 1), row_hot, 1, 0)
 
-    def paired(w_ref):
-        t = jnp.transpose(w_ref[...].astype(F32))
-        return jnp.concatenate([t[:half], t[half:]], axis=1).astype(BF16)
-
-    right_w[:half] = paired(right_gate)
-    right_w[half:] = paired(right_proj)
+    def turned(w_ref):
+        return jnp.transpose(w_ref[...].astype(F32)).astype(BF16)
+
+    right_w[:width] = turned(right_gate)
+    right_w[width:] = turned(right_proj)
+
+    lane = lax.broadcasted_iota(jnp.int32, (rows, width), 1)
+
+    def swap(x, y):
+        return (
+            jnp.where(lane < half, x, pltpu.roll(y, half, 1)),
+            jnp.where(lane < half, pltpu.roll(x, half, 1), y),
+        )
 
     def at_column(k):
         return normed[pl.ds(k, rows, stride=cols), :].astype(BF16)
 
+    def two_columns(k):
+        return jnp.concatenate([at_column(k), at_column(k + 1)], axis=0)
+
     def edges(w_ref, send):
         w = w_ref[...]
-        empty = jnp.zeros((rows, width), BF16)
-
-        @pl.loop(0, cols, unroll=8)
-        def _(k):
-            n = at_column(k)
-            both = jnp.concatenate(
-                [jnp.concatenate([n, empty], axis=1), jnp.concatenate([empty, n], axis=1)], axis=0
-            )
-            pre = contract(w, both, 1, 1)
-            edge = mask[pl.ds(k, 1), :] * jax.nn.sigmoid(pre[:half]) * pre[half:]
-            stage[pl.ds(k, half, stride=cols), :] = edge
+
+        @pl.loop(0, cols // 2, unroll=4)
+        def _(p):
+            k = 2 * p
+            pre = contract(w, two_columns(k), 1, 1)
+            here = jnp.where(lane[:1] < half, mask[pl.ds(k, 1), :], mask[pl.ds(k + 1, 1), :])
+            edge = here * jax.nn.sigmoid(pre[:width]) * pre[width:]
+            one, two = swap(edge[:half], edge[half:])
+            stage[pl.ds(k, half, stride=cols), :] = one
+            stage[pl.ds(k + 1, half, stride=cols), :] = two
 
         @pl.loop(0, half // group)
         def _(g):
@@ -221,11 +230,10 @@
     )
     for q in range(parts):
         each_peer(lambda d: right_copy(d, q).start())
-    left_w[:half] = paired(left_gate)
-    left_w[half:] = paired(left_proj)
+    left_w[:width] = turned(left_gate)
+    left_w[width:] = turned(left_proj)
     right_all[r, :, own_cols, :] = right_send[pl.ds(c * mine, mine)]
 
-    lane = lax.broadcasted_iota(jnp.int32, (rows, width), 1)
 
     def left_over(q, way):
         return pltpu.make_async_remote_copy(
@@ -343,9 +351,9 @@
         pass_on(r, q, 0, False)
         pass_on(r, q, 1, False)
 
-    @pl.loop(0, cols, unroll=8)
-    def _(k):
-        gates[k] = jax.nn.sigmoid(contract(at_column(k), out_gate[...], 1, 0))
+    @pl.loop(0, cols // 2, unroll=4)
+    def _(p):
+        gates[p] = jax.nn.sigmoid(contract(two_columns(2 * p), out_gate[...], 1, 0))
 
     own_on(0)
 
@@ -362,7 +370,6 @@
     s = column(out_shift)
     gain[...] = jnp.where(lane_h < half, g[:half], g[half:])
     shift[...] = jnp.where(lane_h < half, s[:half], s[half:])
-    out_w[...] = jnp.concatenate([out_proj[:half], out_proj[half:]], axis=1)
 
     @pl.when(first | last)
     def _():
@@ -418,12 +425,18 @@
     means[...] = m
     scales[...] = lax.rsqrt(squares / width - m * m + epsilon)
 
-    @pl.loop(0, cols, unroll=8)
-    def _(j):
+    def normed_x(j):
         x = stage[pl.ds(j, half, stride=cols), :]
-        x = (x - means[pl.ds(j, 1), :]) * scales[pl.ds(j, 1), :] * gain[...] + shift[...]
-        y = contract(x.astype(BF16), out_w[...], 0, 0)
-        normed[pl.ds(j, rows, stride=cols), :] = gates[j] * (y[:half, :width] + y[half:, width:])
+        return (x - means[pl.ds(j, 1), :]) * scales[pl.ds(j, 1), :] * gain[...] + shift[...]
+
+    @pl.loop(0, cols // 2, unroll=4)
+    def _(p):
+        j = 2 * p
+        low, high = swap(normed_x(j), normed_x(j + 1))
+        x = jnp.concatenate([low, high], axis=0).astype(BF16)
+        y = gates[p] * contract(x, out_proj[...], 0, 0)
+        normed[pl.ds(j, rows, stride=cols), :] = y[:rows]
+        normed[pl.ds(j + 1, rows, stride=cols), :] = y[rows:]
 
     @pl.loop(0, rows // group)
     def _(g):
@@ -473,7 +486,7 @@
     rows, cols, width = pair.shape
     half = width // 2
     mine = half // nc
-    assert rows == half and nr >= 4 and nr % 2 == 0 and nc % 2 == 0 and nc >= 4 and mine >= 2
+    assert rows == half and cols % 2 == 0 and nr >= 4 and nr % 2 == 0 and nc % 2 == 0 and nc >= 4 and mine >= 2
     sizes = (1,) * mine if mine < 4 else (1,) + (2,) * ((mine - 2) // 2) + (1,) * (1 + mine % 2)
     parts = len(sizes)
     total = cols * nc
@@ -492,15 +505,14 @@
             dma((len(operands),)),
             vmem((rows * cols, width), F32),
             vmem((half * cols, width), F32),
-            vmem((cols, rows, width), F32),
+            vmem((cols // 2, 2 * rows, width), F32),
             vmem((cols, width), F32),
-            vmem((width, 2 * width), BF16),
-            vmem((width, 2 * width), BF16),
+            vmem((2 * width, width), BF16),
+            vmem((2 * width, width), BF16),
             vmem((cols, width), F32),
             vmem((cols, width), F32),
             vmem((half, width), F32),
             vmem((half, width), F32),
-            vmem((half, 2 * width), BF16),
             vmem((half, cols, width), BF16),
             vmem((half, cols, width), BF16),
             vmem((mine, total, width), BF16),

time: 42.2 us -> 43.1 us (1.021)
  Pallas kernels: 41.2 us -> 42.2 us
    pallas_call x1, Pallas kernels: 41.2 us -> 42.2 us  [local(): pl.pallas_call(functools.partial(kernel, nr, nc, sizes), out_shape=jax.Sh...]
where the time goes in v7:
time: 43.1 us; the launch traced here: 43 us
  Pallas kernels  42.2 us (98%)
  local copies, waits for them, and re-layouts  0.8 us (2%)
    pallas_call x1, Pallas kernels, local(): pl.pallas_call(functools.partial(kernel, nr, nc, sizes), out_shape=jax.Sh...  42.2 us

profile of v7, /device:TPU:5, one launch (start us, length us, event | category | flops | bytes accessed | tf_op | source)
XLA Modules:
  0.0 43.0 jit_solution(14797272763358064194)
XLA Ops:
  0.0 42.2 %shard_map.118 = bf16[64,32,128]{2,1,0:T(8,128)(2,1)S(1)} custom-call(bf16[64,32,128]{2,1,0:T(8,128)(2,1)} %refs_0_.1, s32[64,64]{1,0:T(8,128)} %refs_1_.1, f32[1,128]{1,0:T(1,128)} %bitcast.4, f32[1,128]{1,0:T(1,128)} %bitcast.5, bf16[128,128]{1,0:T(8,128)(2,1)} %refs_4_.1, bf16[128,128]{1,0:T(8,128)(2,1)} %refs_5_.1, bf16[128,128]{1,0:T(8,128)(2,1)} %refs_6_.1, ...), custom_call_target="tpu_custom_call" | custom-call | tf_op jit(solution)/shard_map/pallas_call | solution.py:499
  42.2 0.8 %copy.14 = bf16[64,32,128]{2,1,0:T(8,128)(2,1)} copy(bf16[64,32,128]{2,1,0:T(8,128)(2,1)S(1)} %shard_map.118) | data formatting | bytes 1048576
